TPU v7x, 128 devices: a whole 4x4x4 slice. The times are simulated.
128 devices in a mesh: vp: 32 (over z, x, core), cd: 4 (over y).
Axes of the slice: x: 4, y: 4, z: 4, core: 2. Of those that a mesh axis runs over, the one named last changes fastest.
Arguments:
- amplitudes: bfloat16 [64, 65536], P('vp'), may hold values from -6 to 6
- integrals: bfloat16 [131072, 8192], P(('vp', 'cd')), may hold values from -0.046875 to 0.046875
- occ_irrep: int32 [200], replicated, may hold values from 0 to 3
- pair_occ: int32 [64, 2], replicated, may hold values from 0 to 199
- cd_sector: int32 [512], replicated, may hold values from 0 to 3
- ab_sector: int32 [64], replicated, may hold values from 0 to 3, as said below
- block_owner: int32 [512, 1], replicated, may hold values from 0 to 127; in each aligned block of 512 rows (0 to 511, 512 to 1023, ...) at most 8 rows name the same one
Outputs:
- residual: float32 [64, 8192], P('vp', 'cd')
Inputs may be any that keep to these rules, and one draw needn't show every extreme that they name: `block_owner`: each owner index owns at most 8 blocks and at least one; some index owns exactly 8. `ab_sector`: each ab panel of 2048 pairs holds exactly 4 blocks of each of the four sectors.
All inputs are finite; a program needn't handle non-finite values.
Results may differ from a plain program's by a relative error of at most 0.0003.
Values may be sent and summed in bfloat16 or wider, within the bound.
No kernel may reach another device: no remote copies, remote signals or barrier semaphores. Data moves between devices by JAX's collectives and lax.ppermute only.
A program may use at most 64 MiB of HBM per device.

v0:
```python
import jax
import jax.numpy as jnp
from jax import lax
from jax.sharding import PartitionSpec as P

BLK = 128


def pair_symmetry(occ_irrep, pair_occ):
    orbitals = jnp.arange(occ_irrep.shape[0], dtype=jnp.int32)
    first = jnp.sum(jnp.where(pair_occ[:, 0:1] == orbitals[None, :], occ_irrep[None, :], 0), axis=1)
    second = jnp.sum(
        jnp.where(pair_occ[:, 1:2] == orbitals[None, :], occ_irrep[None, :], 0), axis=1
    )
    return jnp.bitwise_xor(first, second)


def slot_positions(block_owner, device_total, slot_count):
    owners = block_owner[:, 0]
    owner_hot = (owners[:, None] == jnp.arange(device_total, dtype=jnp.int32)[None, :]).astype(
        jnp.int32
    )
    earlier = jnp.cumsum(owner_hot, axis=0) - owner_hot
    block_rank = jnp.sum(earlier * owner_hot, axis=1)
    return owners * slot_count + block_rank


def shards(amplitudes, integrals, occ_irrep, pair_occ, cd_sector, ab_sector, block_owner):
    vp_count = lax.axis_size("vp")
    cd_count = lax.axis_size("cd")
    vp_index = lax.axis_index("vp")
    cd_index = lax.axis_index("cd")
    row_count = amplitudes.shape[0]
    slot_count = integrals.shape[0] // BLK
    block_count = cd_sector.shape[0]
    ab_total = integrals.shape[1]
    pair_sym = pair_symmetry(occ_irrep, pair_occ)
    local_sym = lax.dynamic_slice_in_dim(pair_sym, vp_index * row_count, row_count)
    position = slot_positions(block_owner, vp_count * cd_count, slot_count)
    owner_ids = jnp.arange(vp_count, dtype=jnp.int32)[:, None] * cd_count + cd_index
    targets = owner_ids * slot_count + jnp.arange(slot_count, dtype=jnp.int32)[None, :]
    selector = (targets[:, :, None] == position[None, None, :]).astype(jnp.bfloat16)
    allowed = cd_sector[None, :] == local_sym[:, None]
    blocked = amplitudes.reshape(row_count, block_count, BLK)
    masked = jnp.where(allowed[:, :, None], blocked, jnp.zeros_like(blocked))
    outgoing = jnp.einsum(
        "psb,rbk->prsk", selector, masked, preferred_element_type=jnp.float32
    ).astype(jnp.bfloat16)
    outgoing = outgoing.reshape(vp_count, row_count, slot_count * BLK)
    partial_value = jnp.einsum(
        "prk,ka->pra",
        lax.all_to_all(outgoing, "vp", split_axis=0, concat_axis=0, tiled=True),
        integrals,
        preferred_element_type=jnp.float32,
    )
    partial_value = partial_value.reshape(vp_count * row_count, ab_total)
    panel_width = ab_total // cd_count
    panel_blocks = panel_width // BLK
    reduced = lax.psum_scatter(partial_value, "vp", scatter_dimension=0, tiled=True)
    reduced = lax.psum_scatter(reduced, "cd", scatter_dimension=1, tiled=True)
    ab_local = lax.dynamic_slice_in_dim(ab_sector, cd_index * panel_blocks, panel_blocks)
    ab_columns = jnp.repeat(ab_local, BLK, total_repeat_length=panel_width)
    sym_match = local_sym[:, None] == ab_columns[None, :]
    return jnp.where(sym_match, reduced, jnp.zeros_like(reduced))


def solution(mesh):
    return jax.shard_map(
        shards,
        mesh=mesh,
        in_specs=(P("vp", None), P(("vp", "cd"), None), P(), P(), P(), P(), P()),
        out_specs=P("vp", "cd"),
        check_vma=False,
    )
```

profile of v0, /device:TPU:1, one launch (start us, length us, event | category | flops | bytes accessed | tf_op | source)
XLA Modules:
  0.0 207.6 jit_solution(10828203124442087297)
XLA Ops:
  6.5 0.0 all-reduce.3.cloned.1.call-start
  6.5 0.8 copy.19
  7.3 0.2 fusion.11
  7.6 0.9 fusion.9
  8.6 0.7 multiply_add_fusion
  9.3 0.8 slice_bitcast_fusion.2
  10.0 0.9 select_reduce_fusion
  10.9 0.1 dynamic_slice.6
  11.0 0.8 broadcast_compare_fusion
  11.7 1.4 fusion.2
  13.1 0.1 copy.26
  13.2 16.9 %all_to_all.5 = bf16[32,2,1024]{2,1,0:T(2,128)(2,1)S(1)} all-to-all(bf16[32,2,1024]{2,1,0:T(2,128)(2,1)S(1)} %reshape.260), channel_id=1, replica_groups=mesh['vp'=32,'cd'=4] {'vp'}, dimensions={0} | all-to-all | bytes 262144 | tf_op jit(solution)/shard_map/all_to_all | solution.py:52
  30.1 8.8 %fusion = f32[32,2,8192]{2,0,1:T(8,128)S(1)} fusion(bf16[1024,8192]{1,0:T(8,128)(2,1)} %param.10, bf16[32,2,1024]{2,1,0:T(2,128)(2,1)S(1)} %all_to_all.5), kind=kOutput, calls=%fused_computation | convolution fusion | flops 1073741824 | bytes 19005440 | tf_op jit(solution)/shard_map/prk,ka->pra/dot_general | solution.py:50
  38.9 1.6 copy.24
  40.5 2.5 %reshape.188 = f32[64,8192]{1,0:T(8,128)} reshape(f32[32,2,8192]{2,1,0:T(2,128)S(1)} %copy.24) | data formatting | bytes 4194304 | tf_op jit(solution)/shard_map/reshape | solution.py:56
  42.9 0.0 all-reduce.3.cloned.1.call-update
  43.0 0.0 reduce-scatter.4.cloned.1.call-start
  43.0 0.6 copy-done.1
  43.6 0.6 dynamic-slice.6
  44.8 0.0 copy-done
  44.8 0.1 dynamic_slice.7
  44.9 0.7 fusion.21
  45.6 4.3 %compare_select_fusion.1 = (s32[2048,1]{0,1:T(1,128)S(1)}, s32[2048,1]{0,1:T(1,128)S(1)}) fusion(s32[]{:T(128)} %bitcast.15, s32[]{:T(128)} %bitcast.16, s32[]{:T(128)} %bitcast.17, s32[]{:T(128)} %bitcast.18, s32[]{:T(128)} %bitcast.19, s32[]{:T(128)} %bitcast.21, s32[]{:T(128)} %bitcast.20, s32[2048,1]{0,1:T(1,128)S(1)} %bitcast.75, s32[2048,1]{0,1:T(1,128)S(1)} %bitcast.76), kind=kLoop, calls=%fused_computation.37 | loop fusion | flops 28672 | bytes 32796 | tf_op jit(solution)/shard_map/jit(_take)/gather | solution.py:62
  50.0 0.2 compare_reduce_fusion.8
  50.2 98.0 %all-reduce.3.cloned.1.call-done = f32[64,8192]{1,0:T(8,128)} async-done(((f32[64,8192]{1,0:T(8,128)}), f32[64,8192]{1,0:T(8,128)}) %all-reduce.3.cloned.1.call-update) | async-done | bytes 2097168
  148.2 1.0 constant_dynamic-slice_fusion
  149.2 2.6 %copy.27 = f32[2,8192]{0,1:T(8,128)} copy(f32[2,8192]{1,0:T(2,128)S(1)} %constant_dynamic-slice_fusion) | data formatting | bytes 131072
  151.8 0.0 reduce-scatter.4.cloned.1.call-update
  151.8 5.7 %select_select_fusion = s32[2048]{0:T(1024)S(1)} fusion(pred[2048]{0:T(1024)(128)(4,1)S(1)} %get-tuple-element.25, pred[2048]{0:T(1024)(128)(4,1)S(1)} %get-tuple-element.24, pred[2048]{0:T(1024)(128)(4,1)S(1)} %get-tuple-element.23, pred[2048]{0:T(1024)(128)(4,1)S(1)} %get-tuple-element.22, pred[2048]{0:T(1024)(128)(4,1)S(1)} %get-tuple-element.21, ...), kind=kLoop, calls=%fused_computation.45 | loop fusion | flops 36864 | bytes 34852 | tf_op jit(solution)/shard_map/jit(_take)/select_n | solution.py:62
  157.5 41.0 %reduce-scatter.4.cloned.1.call-done = f32[2048,2]{1,0:T(8,128)} async-done(((f32[8192,2]{1,0:T(8,128)}), f32[2048,2]{1,0:T(8,128)}) %reduce-scatter.4.cloned.1.call-update) | async-done | bytes 16400
  198.5 1.6 copy.28
  200.0 0.7 compare_select_fusion.7
  (14 shorter events, 0.2 us)
Async XLA Ops:
  6.5 141.7 %all-reduce.3.cloned.1.call-start = ((), (), s32[]{:S(2)}) async-start(), calls=%async_computation.3 | async-start | bytes 4194304
  42.9 0.7 copy-start.1
  42.9 1.9 copy-start
  43.0 155.5 %reduce-scatter.4.cloned.1.call-start = ((), (), s32[]{:S(2)}) async-start(), calls=%async_computation.2 | async-start | bytes 5242880
Sparse Core Ops, SparseCore 0:
  43.1 105.0 all-reduce.2
  152.0 46.4 reduce-scatter.3
where the time goes:
time: 208 us
  waiting for transfers between devices  139 us (67%)
  blocking collectives  16.9 us (8%)
  other arithmetic  14.4 us (7%)
  between operations  14.2 us (7%)
  local copies, waits for them, and re-layouts  12.9 us (6%)
  matrix products  10.1 us (5%)
    unnamed x4, waiting for transfers between devices  139 us
    all_to_all x1, blocking collectives, shards(): lax.all_to_all(outgoing, 'vp', split_axis=0, concat_axis=0, tiled=True)  16.9 us
    dot_general x1, matrix products, shards(): jnp.einsum('prk,ka->pra', lax.all_to_all(outgoing, 'vp', split_axis=0, co...  8.78 us
    unnamed x9, local copies, waits for them, and re-layouts  6.31 us
    select_n x1, other arithmetic, shards(): ab_columns = jnp.repeat(ab_local, BLK, total_repeat_length=panel_width)  5.66 us
    gather x2, other arithmetic, shards(): ab_columns = jnp.repeat(ab_local, BLK, total_repeat_length=panel_width)  4.55 us
  transfers between devices with their start and end apart: 2, of which 2 were waited for; matrix products, arithmetic and copies ran while one was open for 6% of the time, Pallas kernels for 0%

commit v1 on v0

v1 whole, which is shorter than its diff:
```python
import jax
import jax.numpy as jnp
from jax import lax
from jax.experimental import pallas as pl
from jax.experimental.pallas import tpu as pltpu
from jax.sharding import PartitionSpec as P

BLK = 128
F32 = jnp.float32
BF16 = jnp.bfloat16


def iota(shape, dim):
    return lax.broadcasted_iota(jnp.int32, shape, dim)


def ones_where(mask):
    return jnp.where(mask, 1.0, 0.0).astype(BF16)


def dot(a, b):
    return jnp.dot(a, b, preferred_element_type=F32)


def row_symmetry(occ, pair, row):
    return occ[pair[0, row]] ^ occ[pair[1, row]]


def route_kernel(occ, pair, amp, owner, cd, ab, out, table):
    vp = lax.axis_index("vp")
    y = lax.axis_index("cd")
    nblk = owner.shape[1]
    sym0 = row_symmetry(occ, pair, 2 * vp)
    sym1 = row_symmetry(occ, pair, 2 * vp + 1)
    own = owner[...]
    cdrow = cd[...]
    prow = iota((48, nblk), 0)
    ids = jnp.where(prow < 32, prow, vp) * 4 + y
    hot = own == ids
    before = ones_where(iota((nblk, nblk), 0) < iota((nblk, nblk), 1))
    rank = dot(ones_where(hot), before)
    rank32 = rank[:32]
    hot32 = hot[:32]
    code0 = jnp.where(hot32 & (cdrow == sym0), rank32 * 2.0, -4.0)
    code1 = jnp.where(hot32 & (cdrow == sym1), rank32 * 2.0 + 1.0, -4.0)
    codes = jnp.concatenate([code0, code1], axis=0).astype(BF16)
    widen = ones_where(iota((nblk, 2 * nblk), 0) == (iota((nblk, 2 * nblk), 1) >> 1))
    wide = dot(codes, widen)
    code = jnp.where((iota((32, 2 * nblk), 1) & 1) == 0, wide[:32], wide[32:])
    place = iota((32, 16, 2 * nblk), 1).astype(F32)
    select = ones_where(code[:, None, :] == place).reshape(512, 2 * nblk)
    out[...] = dot(select, amp[...]).astype(BF16)
    mine = jnp.where(hot[32:33], rank[32:33], -1.0)
    at_slot = mine == iota((16, nblk), 0).astype(F32)
    sector = jnp.sum(jnp.where(at_slot, cdrow.astype(F32), 0.0), axis=1, keepdims=True)
    match = ab[...].astype(F32) == sector
    nab = ab.shape[1]
    j0 = iota((nab, nab), 0)
    j1 = iota((nab, nab), 1)
    order = dot(ones_where(match), ones_where((j0 < j1) & ((j0 >> 4) == (j1 >> 4))))
    source = iota((nab, BLK), 0)
    total = jnp.zeros((16, BLK), F32)
    for m in range(4):
        spot = iota((nab, BLK), 1) == (source >> 4) * 4 + m
        value = jnp.where(spot, source.astype(F32), 0.0).astype(BF16)
        total = total + dot(ones_where(match & (order == float(m))), value)
    table[...] = total[:8].astype(jnp.int32)


def contract_kernel(table, recv, integrals, out):
    row = iota((512, 512), 0)
    origin = (row & 31) * 16 + (row >> 6) * 2 + ((row >> 5) & 1)
    a = dot(ones_where(origin == iota((512, 512), 1)), recv[...]).astype(BF16)
    a = jnp.concatenate([a[s * 64:(s + 1) * 64] for s in range(8)], axis=1)
    for pair_at in range(8):
        columns = []
        for half in range(2):
            cb = pair_at * 2 + half
            columns.append(
                jnp.concatenate(
                    [
                        integrals[
                            s * BLK:(s + 1) * BLK,
                            pl.ds(pl.multiple_of(table[s, cb] * BLK, BLK), BLK),
                        ]
                        for s in range(8)
                    ],
                    axis=0,
                )
            )
        result = dot(a, jnp.concatenate(columns, axis=1))
        for half in range(2):
            cb = pair_at * 2 + half
            for r in range(2):
                out[pl.Slice((cb // 4) * 8 + r * 4 + cb % 4, 32, stride=32), :] = result[
                    r * 32:(r + 1) * 32, half * BLK:(half + 1) * BLK
                ]


def collect_kernel(occ, pair, ab, recv, out, total):
    vp = lax.axis_index("vp")
    y = lax.axis_index("cd")
    total[...] = jnp.sum(recv[...], axis=0)
    for r in range(2):
        sym = row_symmetry(occ, pair, 2 * vp + r)
        count = jnp.int32(0)
        for j in range(16):
            hit = ab[y * 16 + j] == sym
            line = total[pl.ds(r * 4 + jnp.minimum(count, 3), 1), :]
            out[r:r + 1, j * BLK:(j + 1) * BLK] = jnp.where(hit, line, 0.0)
            count = count + hit.astype(jnp.int32)


SMEM = pl.BlockSpec(memory_space=pltpu.SMEM)
VMEM = pl.BlockSpec(memory_space=pltpu.VMEM)


def shards(amplitudes, integrals, occ_irrep, pair_occ, cd_sector, ab_sector, block_owner):
    nblk = cd_sector.shape[0]
    amp = amplitudes.reshape(2, nblk, BLK).transpose(1, 0, 2).reshape(2 * nblk, BLK)
    pair = pair_occ.T
    outgoing, table = pl.pallas_call(
        route_kernel,
        out_shape=(
            jax.ShapeDtypeStruct((512, BLK), BF16),
            jax.ShapeDtypeStruct((8, BLK), jnp.int32),
        ),
        in_specs=[SMEM, SMEM, VMEM, VMEM, VMEM, VMEM],
        out_specs=(VMEM, VMEM),
        compiler_params=pltpu.CompilerParams(vmem_limit_bytes=16 << 20),
        name="route",
    )(occ_irrep, pair, amp, block_owner.T, cd_sector[None, :], ab_sector[None, :])
    incoming = lax.all_to_all(
        outgoing.reshape(32, 16, BLK), "vp", split_axis=0, concat_axis=0, tiled=True
    ).reshape(512, BLK)
    partial_value = pl.pallas_call(
        contract_kernel,
        out_shape=jax.ShapeDtypeStruct((1024, BLK), F32),
        in_specs=[SMEM, VMEM, VMEM],
        out_specs=VMEM,
        compiler_params=pltpu.CompilerParams(vmem_limit_bytes=28 << 20),
        name="contract",
    )(table, incoming, pltpu.with_memory_space_constraint(integrals, pltpu.VMEM))
    gathered = lax.all_to_all(
        partial_value.reshape(128, 8, BLK), ("vp", "cd"), split_axis=0, concat_axis=0, tiled=True
    )
    return pl.pallas_call(
        collect_kernel,
        out_shape=jax.ShapeDtypeStruct((2, 2048), F32),
        in_specs=[SMEM, SMEM, SMEM, VMEM],
        out_specs=VMEM,
        scratch_shapes=[pltpu.VMEM((8, BLK), F32)],
        compiler_params=pltpu.CompilerParams(vmem_limit_bytes=8 << 20),
        name="collect",
    )(occ_irrep, pair, ab_sector, gathered)


def solution(mesh):
    return jax.shard_map(
        shards,
        mesh=mesh,
        in_specs=(P("vp", None), P(("vp", "cd"), None), P(), P(), P(), P(), P()),
        out_specs=P("vp", "cd"),
        check_vma=False,
    )
```

time: 208 us -> 52.1 us (0.25)
  waiting for transfers between devices: 139 us -> 0 us
  blocking collectives: 16.9 us -> 36.3 us
  other arithmetic: 14.4 us -> 0 us
  between operations: 14.2 us -> 0.03 us
  matrix products: 10.1 us -> 0 us
  Pallas kernels: 0 us -> 5.32 us
  local copies, waits for them, and re-layouts: 12.9 us -> 10.1 us
    unnamed x4 -> x0, waiting for transfers between devices: 139 us -> none
    all_to_all x1 -> x2, blocking collectives: 16.9 us -> 36.3 us  [the longest x1 19.5 us: shards(): lax.all_to_all(partial_value.reshape(128, 8, BLK), ('vp', 'cd'), split_ax...]
    dot_general x2 -> x0, matrix products: 10.1 us -> none  [the longest x1 8.78 us: shards(): jnp.einsum('prk,ka->pra', lax.all_to_all(outgoing, 'vp', split_axis=0, co...]
    select_n x2 -> x0, other arithmetic: 6.35 us -> none  [the longest x1 5.66 us: shards(): ab_columns = jnp.repeat(ab_local, BLK, total_repeat_length=panel_width)]
    pallas_call x0 -> x3, Pallas kernels: none -> 5.32 us  [the longest x1 2.4 us: shards(): pl.pallas_call(contract_kernel, out_shape=jax.ShapeDtypeStruct((1024, BLK...]
    gather x2 -> x0, other arithmetic: 4.55 us -> none  [shards(): ab_columns = jnp.repeat(ab_local, BLK, total_repeat_length=panel_width)]
    unnamed x9 -> x20, local copies, waits for them, and re-layouts: 6.31 us -> 10.1 us
    reshape x3 -> x0, local copies, waits for them, and re-layouts: 2.54 us -> none  [the longest x1 2.45 us: shards(): partial_value = partial_value.reshape(vp_count * row_count, ab_total)]
  transfers between devices with their start and end apart: 2 -> 0, of which waited for: 2 -> 0; matrix products, arithmetic and copies ran while one was open for 6% -> 0% of each run, Pallas kernels for 0% -> 0%
where the time goes in v1:
time: 52.1 us; the launch traced here: 51.8 us
  blocking collectives  36.3 us (70%)
  local copies, waits for them, and re-layouts  10.1 us (19%)
  Pallas kernels  5.32 us (10%)
    all_to_all x1, blocking collectives, shards(): lax.all_to_all(partial_value.reshape(128, 8, BLK), ('vp', 'cd'), split_ax...  19.5 us
    all_to_all x1, blocking collectives, shards(): lax.all_to_all(outgoing.reshape(32, 16, BLK), 'vp', split_axis=0, concat_...  16.8 us
    unnamed x20, local copies, waits for them, and re-layouts  10.1 us
    pallas_call x1, Pallas kernels, shards(): pl.pallas_call(contract_kernel, out_shape=jax.ShapeDtypeStruct((1024, BLK...  2.4 us
    pallas_call x1, Pallas kernels, shards(): pl.pallas_call(route_kernel, out_shape=(jax.ShapeDtypeStruct((512, BLK),...  1.59 us
    pallas_call x1, Pallas kernels, shards(): pl.pallas_call(collect_kernel, out_shape=jax.ShapeDtypeStruct((2, 2048),...  1.33 us

profile of v1, /device:TPU:1, one launch (start us, length us, event | category | flops | bytes accessed | tf_op | source)
XLA Modules:
  0.0 51.8 jit_solution(5216142996653655351)
XLA Ops:
  0.0 0.0 copy-start.3
  0.0 0.0 copy-start.9
  0.0 0.0 copy-start.5
  0.0 0.0 copy-start.1
  0.0 1.0 %copy-done.1 = bf16[2,65536]{1,0:T(2,128)(2,1)S(1)} copy-done((bf16[2,65536]{1,0:T(2,128)(2,1)S(1)}, bf16[2,65536]{1,0:T(2,128)(2,1)}, u32[]{:S(2)}) %copy-start.1) | copy-done | bytes 262168
  1.0 0.0 copy-start.2
  1.0 0.7 %copy-done.2 = s32[200]{0:T(256)S(1)} copy-done((s32[200]{0:T(256)S(1)}, s32[200]{0:T(256)}, u32[]{:S(2)}) %copy-start.2) | copy-done | bytes 824
  1.7 0.0 copy-start.4
  1.7 0.7 %copy-done.4 = s32[64,2]{0,1:T(2,128)S(1)} copy-done((s32[64,2]{0,1:T(2,128)S(1)}, s32[64,2]{0,1:T(2,128)}, u32[]{:S(2)}) %copy-start.4) | copy-done | bytes 536
  2.4 0.0 copy-start.6
  2.4 0.7 %copy-done.6 = s32[512,1]{0,1:T(1,128)S(1)} copy-done((s32[512,1]{0,1:T(1,128)S(1)}, s32[512,1]{0,1:T(1,128)}, u32[]{:S(2)}) %copy-start.6) | copy-done | bytes 2072
  3.0 0.0 copy-start.7
  3.0 0.7 %copy-done.7 = s32[512]{0:T(512)S(1)} copy-done((s32[512]{0:T(512)S(1)}, s32[512]{0:T(512)}, u32[]{:S(2)}) %copy-start.7) | copy-done | bytes 2072
  3.7 0.0 copy-start.8
  3.7 0.7 %copy-done.8 = s32[64]{0:T(128)S(1)} copy-done((s32[64]{0:T(128)S(1)}, s32[64]{0:T(128)}, u32[]{:S(2)}) %copy-start.8) | copy-done | bytes 280
  4.4 1.6 %route.1 = (bf16[512,128]{1,0:T(8,128)(2,1)S(1)}, s32[8,128]{1,0:T(8,128)S(1)}) custom-call(s32[200]{0:T(256)S(1)} %copy-done.2, s32[2,64]{1,0:T(2,128)S(1)} %bitcast.16, bf16[1024,128]{1,0:T(8,128)(2,1)S(1)} %bitcast.14, s32[1,512]{1,0:T(1,128)S(1)} %bitcast.18, s32[1,512]{1,0:T(1,128)S(1)} %bitcast.19, s32[1,64]{1,0:T(1,128)S(1)} %bitcast.20), custom_call_target="tpu_custom_call" | custom-call | tf_op jit(solution)/shard_map/route/pallas_call | solution.py:122
  6.0 16.8 %all_to_all.10 = bf16[32,16,128]{2,1,0:T(8,128)(2,1)S(1)} all-to-all(bf16[32,16,128]{2,1,0:T(8,128)(2,1)S(1)} %bitcast.15), channel_id=1, replica_groups=mesh['vp'=32,'cd'=4] {'vp'}, dimensions={0} | all-to-all | bytes 262144 | tf_op jit(solution)/shard_map/all_to_all | solution.py:133
  22.8 0.0 copy-start
  22.8 5.8 %copy-done = bf16[1024,8192]{1,0:T(8,128)(2,1)S(1)} copy-done((bf16[1024,8192]{1,0:T(8,128)(2,1)S(1)}, bf16[1024,8192]{1,0:T(8,128)(2,1)}, u32[]{:S(2)}) %copy-start) | copy-done | bytes 16777240
  28.6 2.4 %contract.1 = f32[1024,128]{1,0:T(8,128)S(1)} custom-call(s32[8,128]{1,0:T(8,128)S(1)} %get-tuple-element.7.table, bf16[512,128]{1,0:T(8,128)(2,1)S(1)} %bitcast.13, bf16[1024,8192]{1,0:T(8,128)(2,1)S(1)} %copy-done), custom_call_target="tpu_custom_call" | custom-call | tf_op jit(solution)/shard_map/contract/pallas_call | solution.py:136
  31.0 19.5 %all_to_all.11.recv = f32[128,8,128]{2,1,0:T(8,128)S(1)} all-to-all(f32[128,8,128]{2,1,0:T(8,128)S(1)} %bitcast.12), channel_id=1, replica_groups=mesh['vp'=32,'cd'=4] {'vp','cd'}, dimensions={0} | all-to-all | bytes 1048576 | tf_op jit(solution)/shard_map/all_to_all | solution.py:144
  50.5 0.0 copy-done.3
  50.5 0.0 copy-done.9
  50.5 0.0 copy-done.5
  50.5 1.3 %collect.1 = f32[2,2048]{1,0:T(2,128)} custom-call(s32[200]{0:T(256)S(1)} %copy-done.3, s32[2,64]{1,0:T(2,128)S(1)} %bitcast.17, s32[64]{0:T(128)S(1)} %copy-done.9, f32[128,8,128]{2,1,0:T(8,128)S(1)} %all_to_all.11.recv), custom_call_target="tpu_custom_call" | custom-call | tf_op jit(solution)/shard_map/collect/pallas_call | solution.py:147
Async XLA Ops:
  0.0 50.5 %copy-start.3 = (s32[200]{0:T(256)S(1)}, s32[200]{0:T(256)}, u32[]{:S(2)}) copy-start(s32[200]{0:T(256)} %occ.3) | copy-start | bytes 2404
  0.0 50.5 %copy-start.9 = (s32[64]{0:T(128)S(1)}, s32[64]{0:T(128)}, u32[]{:S(2)}) copy-start(s32[64]{0:T(128)} %ab.1) | copy-start | bytes 772
  0.0 50.5 %copy-start.5 = (s32[64,2]{0,1:T(2,128)S(1)}, s32[64,2]{0,1:T(2,128)}, u32[]{:S(2)}) copy-start(s32[64,2]{0,1:T(2,128)} %param.10) | copy-start | bytes 1540
  0.0 1.0 %copy-start.1 = (bf16[2,65536]{1,0:T(2,128)(2,1)S(1)}, bf16[2,65536]{1,0:T(2,128)(2,1)}, u32[]{:S(2)}) copy-start(bf16[2,65536]{1,0:T(2,128)(2,1)} %param.7) | copy-start | bytes 786436
  1.0 0.7 %copy-start.2 = (s32[200]{0:T(256)S(1)}, s32[200]{0:T(256)}, u32[]{:S(2)}) copy-start(s32[200]{0:T(256)} %occ.3) | copy-start | bytes 2404
  1.7 0.7 %copy-start.4 = (s32[64,2]{0,1:T(2,128)S(1)}, s32[64,2]{0,1:T(2,128)}, u32[]{:S(2)}) copy-start(s32[64,2]{0,1:T(2,128)} %param.10) | copy-start | bytes 1540
  2.4 0.7 %copy-start.6 = (s32[512,1]{0,1:T(1,128)S(1)}, s32[512,1]{0,1:T(1,128)}, u32[]{:S(2)}) copy-start(s32[512,1]{0,1:T(1,128)} %param.13) | copy-start | bytes 6148
  3.0 0.7 %copy-start.7 = (s32[512]{0:T(512)S(1)}, s32[512]{0:T(512)}, u32[]{:S(2)}) copy-start(s32[512]{0:T(512)} %param.11) | copy-start | bytes 6148
  3.7 0.7 %copy-start.8 = (s32[64]{0:T(128)S(1)}, s32[64]{0:T(128)}, u32[]{:S(2)}) copy-start(s32[64]{0:T(128)} %ab.1) | copy-start | bytes 772
  22.8 5.8 %copy-start = (bf16[1024,8192]{1,0:T(8,128)(2,1)S(1)}, bf16[1024,8192]{1,0:T(8,128)(2,1)}, u32[]{:S(2)}) copy-start(bf16[1024,8192]{1,0:T(8,128)(2,1)} %integrals.1) | copy-start | bytes 50331652

commit v2 on v1

v2 whole, which is shorter than its diff:
```python
import jax
import jax.numpy as jnp
from jax import lax
from jax.experimental import pallas as pl
from jax.experimental.pallas import tpu as pltpu
from jax.sharding import PartitionSpec as P

BLK = 128
F32 = jnp.float32
BF16 = jnp.bfloat16


def iota(shape, dim):
    return lax.broadcasted_iota(jnp.int32, shape, dim)


def ones_where(mask):
    return jnp.where(mask, 1.0, 0.0).astype(BF16)


def dot(a, b):
    return jnp.dot(a, b, preferred_element_type=F32)


def row_symmetry(occ, pair, row):
    return occ[pair[0, row]] ^ occ[pair[1, row]]


def fetch(sems, *pairs):
    copies = [pltpu.make_async_copy(src, dst, sems.at[i]) for i, (src, dst) in enumerate(pairs)]
    for copy in copies:
        copy.start()
    return copies


def route_kernel(
    occ_h, pair_h, amp_h, owner_h, cd_h, ab_h, integrals, out, blocks,
    occ, pair, amp, owner, cd, ab, table_v, table, sems, row_sems,
):
    copies = fetch(
        sems, (owner_h, owner), (cd_h, cd), (ab_h, ab), (occ_h, occ), (pair_h, pair), (amp_h, amp)
    )
    vp = lax.axis_index("vp")
    y = lax.axis_index("cd")
    nblk = owner.shape[1]
    nab = ab.shape[1]
    before = ones_where(iota((nblk, nblk), 0) < iota((nblk, nblk), 1))
    widen = ones_where(iota((nblk, 2 * nblk), 0) == (iota((nblk, 2 * nblk), 1) >> 1))
    for copy in copies[:5]:
        copy.wait()
    cdrow = cd[...]
    prow = iota((48, nblk), 0)
    hot = owner[...] == jnp.where(prow < 32, prow, vp) * 4 + y
    rank = dot(ones_where(hot), before)
    mine = jnp.where(hot[32:], rank[32:], -1.0)
    at_slot = mine == iota((16, nblk), 0).astype(F32)
    sector = jnp.sum(jnp.where(at_slot, cdrow.astype(F32), 0.0), axis=1, keepdims=True)
    match = ab[...].astype(F32) == sector
    j0 = iota((nab, nab), 0)
    j1 = iota((nab, nab), 1)
    order = dot(ones_where(match), ones_where((j0 < j1) & ((j0 >> 4) == (j1 >> 4))))
    source = iota((nab, BLK), 0)
    total = jnp.zeros((16, BLK), F32)
    for m in range(4):
        spot = iota((nab, BLK), 1) == (source >> 4) * 4 + m
        value = jnp.where(spot, source.astype(F32), 0.0).astype(BF16)
        total = total + dot(ones_where(match & (order == float(m))), value)
    table_v[...] = total[:8].astype(jnp.int32)
    to_scalars = pltpu.make_async_copy(table_v, table, sems.at[0])
    to_scalars.start()
    sym0 = row_symmetry(occ, pair, 2 * vp)
    sym1 = row_symmetry(occ, pair, 2 * vp + 1)
    code0 = jnp.where(hot[:32] & (cdrow == sym0), rank[:32] * 2.0, -4.0)
    code1 = jnp.where(hot[:32] & (cdrow == sym1), rank[:32] * 2.0 + 1.0, -4.0)
    codes = jnp.concatenate([code0, code1], axis=0).astype(BF16)
    wide = dot(codes, widen)
    code = jnp.where((iota((32, 2 * nblk), 1) & 1) == 0, wide[:32], wide[32:])
    to_scalars.wait()

    for s in range(8):
        for cb in range(16):
            start = pl.multiple_of(table[s, cb] * BLK, BLK)
            pltpu.make_async_copy(
                integrals.at[s * BLK:(s + 1) * BLK, pl.ds(start, BLK)],
                blocks.at[s * BLK:(s + 1) * BLK, cb * BLK:(cb + 1) * BLK],
                row_sems.at[s],
            ).start()
    place = iota((32, 16, 2 * nblk), 1).astype(F32)
    select = ones_where(code[:, None, :] == place).reshape(512, 2 * nblk)
    copies[5].wait()
    out[...] = dot(select, amp[...]).astype(BF16)
    for s in range(8):
        rows = blocks.at[s * BLK:(s + 1) * BLK, :]
        pltpu.make_async_copy(rows, rows, row_sems.at[s]).wait()


def contract_kernel(recv, blocks, out):
    row = iota((512, 512), 0)
    origin = (row & 31) * 16 + (row >> 6) * 2 + ((row >> 5) & 1)
    a = dot(ones_where(origin == iota((512, 512), 1)), recv[...]).astype(BF16)
    a = jnp.concatenate([a[s * 64:(s + 1) * 64] for s in range(8)], axis=1)
    for pair_at in range(8):
        result = dot(a, blocks[:, pair_at * 256:(pair_at + 1) * 256])
        for half in range(2):
            cb = pair_at * 2 + half
            for r in range(2):
                out[pl.Slice((cb // 4) * 8 + r * 4 + cb % 4, 32, stride=32), :] = result[
                    r * 32:(r + 1) * 32, half * BLK:(half + 1) * BLK
                ]


def collect_kernel(occ, pair, ab, recv, out, total):
    vp = lax.axis_index("vp")
    y = lax.axis_index("cd")
    total[...] = jnp.sum(recv[...], axis=0)
    for r in range(2):
        sym = row_symmetry(occ, pair, 2 * vp + r)
        count = jnp.int32(0)
        for j in range(16):
            hit = ab[y * 16 + j] == sym
            line = total[pl.ds(r * 4 + jnp.minimum(count, 3), 1), :]
            out[r:r + 1, j * BLK:(j + 1) * BLK] = jnp.where(hit, line, 0.0)
            count = count + hit.astype(jnp.int32)


SMEM = pl.BlockSpec(memory_space=pltpu.SMEM)
VMEM = pl.BlockSpec(memory_space=pltpu.VMEM)
HBM = pl.BlockSpec(memory_space=pltpu.HBM)


def hbm(*arrays):
    return [pltpu.with_memory_space_constraint(a, pltpu.HBM) for a in arrays]


def shards(amplitudes, integrals, occ_irrep, pair_occ, cd_sector, ab_sector, block_owner):
    nblk = cd_sector.shape[0]
    amp = amplitudes.reshape(2, nblk, BLK).transpose(1, 0, 2).reshape(2 * nblk, BLK)
    pair = pair_occ.T
    owner, cd, ab = block_owner.T, cd_sector[None, :], ab_sector[None, :]
    outgoing, blocks = pl.pallas_call(
        route_kernel,
        out_shape=(
            jax.ShapeDtypeStruct((512, BLK), BF16),
            pltpu.VMEM((1024, 2048), BF16),
        ),
        in_specs=[HBM] * 7,
        out_specs=(VMEM, VMEM),
        scratch_shapes=[
            pltpu.SMEM(occ_irrep.shape, jnp.int32),
            pltpu.SMEM(pair.shape, jnp.int32),
            pltpu.VMEM(amp.shape, BF16),
            pltpu.VMEM(owner.shape, jnp.int32),
            pltpu.VMEM(cd.shape, jnp.int32),
            pltpu.VMEM(ab.shape, jnp.int32),
            pltpu.VMEM((8, BLK), jnp.int32),
            pltpu.SMEM((8, BLK), jnp.int32),
            pltpu.SemaphoreType.DMA((6,)),
            pltpu.SemaphoreType.DMA((8,)),
        ],
        compiler_params=pltpu.CompilerParams(vmem_limit_bytes=16 << 20),
        name="route",
    )(*hbm(occ_irrep, pair, amp, owner, cd, ab, integrals))
    incoming = lax.all_to_all(
        outgoing.reshape(32, 16, BLK), "vp", split_axis=0, concat_axis=0, tiled=True
    ).reshape(512, BLK)
    partial_value = pl.pallas_call(
        contract_kernel,
        out_shape=jax.ShapeDtypeStruct((1024, BLK), F32),
        in_specs=[VMEM, VMEM],
        out_specs=VMEM,
        compiler_params=pltpu.CompilerParams(vmem_limit_bytes=28 << 20),
        name="contract",
    )(incoming, pltpu.with_memory_space_constraint(blocks, pltpu.VMEM))
    gathered = lax.all_to_all(
        partial_value.reshape(128, 8, BLK), ("vp", "cd"), split_axis=0, concat_axis=0, tiled=True
    )
    return pl.pallas_call(
        collect_kernel,
        out_shape=jax.ShapeDtypeStruct((2, 2048), F32),
        in_specs=[SMEM, SMEM, SMEM, VMEM],
        out_specs=VMEM,
        scratch_shapes=[pltpu.VMEM((8, BLK), F32)],
        compiler_params=pltpu.CompilerParams(vmem_limit_bytes=8 << 20),
        name="collect",
    )(occ_irrep, pair, ab_sector, gathered)


def solution(mesh):
    return jax.shard_map(
        shards,
        mesh=mesh,
        in_specs=(P("vp", None), P(("vp", "cd"), None), P(), P(), P(), P(), P()),
        out_specs=P("vp", "cd"),
        check_vma=False,
    )
```

time: 52.1 us -> 43.8 us (0.84)
  local copies, waits for them, and re-layouts: 10.1 us -> 0.01 us
  Pallas kernels: 5.32 us -> 7.1 us
    unnamed x20 -> x6, local copies, waits for them, and re-layouts: 10.1 us -> 0.01 us
    pallas_call x1, Pallas kernels: 1.59 us -> 4.38 us  [shards(): pl.pallas_call(route_kernel, out_shape=(jax.ShapeDtypeStruct((512, BLK),...]
    pallas_call x1, Pallas kernels: 2.4 us -> 1.39 us  [shards(): pl.pallas_call(contract_kernel, out_shape=jax.ShapeDtypeStruct((1024, BLK...]
where the time goes in v2:
time: 43.8 us; the launch traced here: 43.5 us
  blocking collectives  36.3 us (83%)
  Pallas kernels  7.1 us (16%)
    all_to_all x1, blocking collectives, shards(): lax.all_to_all(partial_value.reshape(128, 8, BLK), ('vp', 'cd'), split_ax...  19.5 us
    all_to_all x1, blocking collectives, shards(): lax.all_to_all(outgoing.reshape(32, 16, BLK), 'vp', split_axis=0, concat_...  16.9 us
    pallas_call x1, Pallas kernels, shards(): pl.pallas_call(route_kernel, out_shape=(jax.ShapeDtypeStruct((512, BLK),...  4.38 us
    pallas_call x1, Pallas kernels, shards(): pl.pallas_call(contract_kernel, out_shape=jax.ShapeDtypeStruct((1024, BLK...  1.39 us
    pallas_call x1, Pallas kernels, shards(): pl.pallas_call(collect_kernel, out_shape=jax.ShapeDtypeStruct((2, 2048),...  1.33 us

profile of v2, /device:TPU:1, one launch (start us, length us, event | category | flops | bytes accessed | tf_op | source)
XLA Modules:
  0.0 43.5 jit_solution(15192926866974521170)
XLA Ops:
  0.0 0.0 copy-start
  0.0 0.0 copy-start.2
  0.0 0.0 copy-start.1
  0.0 4.4 %route.1 = (bf16[512,128]{1,0:T(8,128)(2,1)S(1)}, bf16[1024,2048]{1,0:T(8,128)(2,1)S(1)}) custom-call(s32[200]{0:T(256)} %occ.1, s32[2,64]{1,0:T(2,128)} %bitcast.15, bf16[1024,128]{1,0:T(8,128)(2,1)} %bitcast.18, s32[1,512]{1,0:T(1,128)} %bitcast.19, s32[1,512]{1,0:T(1,128)} %bitcast.20, s32[1,64]{1,0:T(1,128)} %bitcast.17, bf16[1024,8192]{1,0:T(8,128)(2,1)} %integrals.1), custom_call_target="tpu_custom_call" | custom-call | tf_op jit(solution)/shard_map/route/pallas_call | solution.py:140
  4.4 16.9 %all_to_all.10 = bf16[32,16,128]{2,1,0:T(8,128)(2,1)S(1)} all-to-all(bf16[32,16,128]{2,1,0:T(8,128)(2,1)S(1)} %bitcast.14), channel_id=1, replica_groups=mesh['vp'=32,'cd'=4] {'vp'}, dimensions={0} | all-to-all | bytes 262144 | tf_op jit(solution)/shard_map/all_to_all | solution.py:163
  21.3 1.4 %contract.1 = f32[1024,128]{1,0:T(8,128)S(1)} custom-call(bf16[512,128]{1,0:T(8,128)(2,1)S(1)} %bitcast.13, bf16[1024,2048]{1,0:T(8,128)(2,1)S(1)} %get-tuple-element.8.blocks), custom_call_target="tpu_custom_call" | custom-call | tf_op jit(solution)/shard_map/contract/pallas_call | solution.py:166
  22.7 19.5 %all_to_all.11.recv = f32[128,8,128]{2,1,0:T(8,128)S(1)} all-to-all(f32[128,8,128]{2,1,0:T(8,128)S(1)} %bitcast.12), channel_id=1, replica_groups=mesh['vp'=32,'cd'=4] {'vp','cd'}, dimensions={0} | all-to-all | bytes 1048576 | tf_op jit(solution)/shard_map/all_to_all | solution.py:174
  42.1 0.0 copy-done
  42.1 0.0 copy-done.2
  42.1 0.0 copy-done.1
  42.1 1.3 %collect.1 = f32[2,2048]{1,0:T(2,128)} custom-call(s32[200]{0:T(256)S(1)} %copy-done, s32[2,64]{1,0:T(2,128)S(1)} %bitcast.16, s32[64]{0:T(128)S(1)} %copy-done.2, f32[128,8,128]{2,1,0:T(8,128)S(1)} %all_to_all.11.recv), custom_call_target="tpu_custom_call" | custom-call | tf_op jit(solution)/shard_map/collect/pallas_call | solution.py:177
Async XLA Ops:
  0.0 42.1 %copy-start = (s32[200]{0:T(256)S(1)}, s32[200]{0:T(256)}, u32[]{:S(2)}) copy-start(s32[200]{0:T(256)} %occ.1) | copy-start | bytes 2404
  0.0 42.1 %copy-start.2 = (s32[64]{0:T(128)S(1)}, s32[64]{0:T(128)}, u32[]{:S(2)}) copy-start(s32[64]{0:T(128)} %ab.1) | copy-start | bytes 772
  0.0 42.1 %copy-start.1 = (s32[64,2]{0,1:T(2,128)S(1)}, s32[64,2]{0,1:T(2,128)}, u32[]{:S(2)}) copy-start(s32[64,2]{0,1:T(2,128)} %param.10) | copy-start | bytes 1540

commit v3 on v2

v3 whole, which is shorter than its diff:
```python
import jax
import jax.numpy as jnp
from jax import lax
from jax.experimental import pallas as pl
from jax.experimental.pallas import tpu as pltpu
from jax.sharding import PartitionSpec as P

BLK = 128
F32 = jnp.float32
BF16 = jnp.bfloat16


def iota(shape, dim):
    return lax.broadcasted_iota(jnp.int32, shape, dim)


def ones_where(mask):
    return jnp.where(mask, 1.0, 0.0).astype(BF16)


def dot(a, b):
    return jnp.dot(a, b, preferred_element_type=F32)


def row_symmetry(occ, pair, row):
    return occ[pair[0, row]] ^ occ[pair[1, row]]


def fetch(sems, *pairs):
    copies = [pltpu.make_async_copy(src, dst, sems.at[i]) for i, (src, dst) in enumerate(pairs)]
    for copy in copies:
        copy.start()
    return copies


def route_kernel(
    occ_h, pair_h, amp_h, owner_h, cd_h, ab_h, integrals, out, blocks, spread,
    occ, pair, amp, owner, cd, ab, lists_v, lists, sems, row_sems,
):
    copies = fetch(
        sems, (owner_h, owner), (cd_h, cd), (ab_h, ab), (occ_h, occ), (pair_h, pair), (amp_h, amp)
    )
    vp = lax.axis_index("vp")
    y = lax.axis_index("cd")
    nblk = owner.shape[1]
    nab = ab.shape[1]
    half_col = iota((nblk, 2 * nblk), 1) >> 1
    before = ones_where(iota((nblk, nblk), 0) < iota((nblk, nblk), 1))
    before2 = ones_where(iota((nblk, 2 * nblk), 0) < half_col)
    widen = ones_where(iota((nblk, 2 * nblk), 0) == half_col)
    j0 = iota((nab, nab), 0)
    j1 = iota((nab, nab), 1)
    within = ones_where((j0 < j1) & ((j0 >> 4) == (j1 >> 4)))
    for copy in copies[:5]:
        copy.wait()
    own = owner[...]
    cdf = cd[...].astype(F32)
    hot = own == vp * 4 + y
    rank = dot(jnp.broadcast_to(ones_where(hot), (16, nblk)), before)[:1]
    mine = jnp.where(hot, rank, -1.0)
    sym0 = row_symmetry(occ, pair, 2 * vp)
    sym1 = row_symmetry(occ, pair, 2 * vp + 1)
    row = iota((16, 1), 0)
    wanted = jnp.where(row < 8, row, jnp.where(row < 12, sym0, sym1))
    match = ab[...] == wanted
    order = dot(ones_where(match), within)
    source = iota((nab, BLK), 0)
    total = jnp.zeros((16, BLK), F32)
    for m in range(4):
        spot = iota((nab, BLK), 1) == (source >> 4) * 4 + m
        value = jnp.where(spot, source.astype(F32), 0.0).astype(BF16)
        total = total + dot(ones_where(match & (order == float(m))), value)
    lists_v[...] = total[:8].astype(jnp.int32)
    to_scalars = pltpu.make_async_copy(lists_v, lists, sems.at[0])
    to_scalars.start()
    sector = [
        jnp.sum(jnp.where(mine == float(s), cdf, 0.0)).astype(jnp.int32) for s in range(8)
    ]
    hot32 = own == iota((32, nblk), 0) * 4 + y
    rank2 = dot(ones_where(hot32), before2)
    both = jnp.concatenate([own.astype(F32), cdf, jnp.zeros((14, nblk), F32)], axis=0)
    wide = dot(both.astype(BF16), widen)
    parity = iota((1, 2 * nblk), 1) & 1
    sym = jnp.where(parity == 0, sym0, sym1).astype(F32)
    ids = (iota((32, 1), 0) * 4 + y).astype(F32)
    keep = (wide[:1] == ids) & (wide[1:2] == sym)
    code = jnp.where(keep, rank2 * 2.0 + parity.astype(F32), -1.0)
    to_scalars.wait()
    for s in range(8):
        for cb in range(16):
            start = pl.multiple_of(lists[sector[s], cb] * BLK, BLK)
            pltpu.make_async_copy(
                integrals.at[s * BLK:(s + 1) * BLK, pl.ds(start, BLK)],
                blocks.at[s * BLK:(s + 1) * BLK, cb * BLK:(cb + 1) * BLK],
                row_sems.at[s],
            ).start()
    place = iota((32, 16, 2 * nblk), 1).astype(F32)
    select = ones_where(code[:, None, :] == place).reshape(512, 2 * nblk)
    shift = iota((nab, BLK), 0) == iota((nab, BLK), 1) + y * 16
    places = match & (order == (row & 3).astype(F32))
    spread[...] = dot(ones_where(places), ones_where(shift))[8:]
    copies[5].wait()
    out[...] = dot(select, amp[...]).astype(BF16)
    for s in range(8):
        rows = blocks.at[s * BLK:(s + 1) * BLK, :]
        pltpu.make_async_copy(rows, rows, row_sems.at[s]).wait()


def contract_kernel(recv, blocks, out, wide):
    wide[...] = recv[...].astype(F32)
    slots = []
    for s in range(8):
        rows = [wide[pl.Slice(s * 2 + r, 32, stride=16), :] for r in range(2)]
        slots.append(jnp.concatenate(rows, axis=0).astype(BF16))
    a = jnp.concatenate(slots, axis=1)
    for pair_at in range(8):
        result = dot(a, blocks[:, pair_at * 256:(pair_at + 1) * 256])
        for half in range(2):
            cb = pair_at * 2 + half
            for r in range(2):
                out[pl.Slice((cb // 4) * 8 + r * 4 + cb % 4, 32, stride=32), :] = result[
                    r * 32:(r + 1) * 32, half * BLK:(half + 1) * BLK
                ]


def collect_kernel(spread, recv, out):
    total = jnp.sum(recv[...], axis=0)
    places = spread[...]
    for j in range(16):
        line = jnp.where(places[:, j:j + 1] > 0.0, total, 0.0)
        out[0:1, j * BLK:(j + 1) * BLK] = jnp.sum(line[:4], axis=0, keepdims=True)
        out[1:2, j * BLK:(j + 1) * BLK] = jnp.sum(line[4:], axis=0, keepdims=True)


VMEM = pl.BlockSpec(memory_space=pltpu.VMEM)
HBM = pl.BlockSpec(memory_space=pltpu.HBM)


def hbm(*arrays):
    return [pltpu.with_memory_space_constraint(a, pltpu.HBM) for a in arrays]


def shards(amplitudes, integrals, occ_irrep, pair_occ, cd_sector, ab_sector, block_owner):
    nblk = cd_sector.shape[0]
    amp = amplitudes.reshape(2, nblk, BLK).transpose(1, 0, 2).reshape(2 * nblk, BLK)
    pair = pair_occ.T
    owner, cd, ab = block_owner.T, cd_sector[None, :], ab_sector[None, :]
    outgoing, blocks, spread = pl.pallas_call(
        route_kernel,
        out_shape=(
            jax.ShapeDtypeStruct((512, BLK), BF16),
            pltpu.VMEM((1024, 2048), BF16),
            jax.ShapeDtypeStruct((8, BLK), F32),
        ),
        in_specs=[HBM] * 7,
        out_specs=(VMEM, VMEM, VMEM),
        scratch_shapes=[
            pltpu.SMEM(occ_irrep.shape, jnp.int32),
            pltpu.SMEM(pair.shape, jnp.int32),
            pltpu.VMEM(amp.shape, BF16),
            pltpu.VMEM(owner.shape, jnp.int32),
            pltpu.VMEM(cd.shape, jnp.int32),
            pltpu.VMEM(ab.shape, jnp.int32),
            pltpu.VMEM((8, BLK), jnp.int32),
            pltpu.SMEM((8, BLK), jnp.int32),
            pltpu.SemaphoreType.DMA((6,)),
            pltpu.SemaphoreType.DMA((8,)),
        ],
        compiler_params=pltpu.CompilerParams(vmem_limit_bytes=16 << 20),
        name="route",
    )(*hbm(occ_irrep, pair, amp, owner, cd, ab, integrals))
    incoming = lax.all_to_all(
        outgoing.reshape(32, 16, BLK), "vp", split_axis=0, concat_axis=0, tiled=True
    ).reshape(512, BLK)
    partial_value = pl.pallas_call(
        contract_kernel,
        out_shape=jax.ShapeDtypeStruct((1024, BLK), F32),
        in_specs=[VMEM, VMEM],
        out_specs=VMEM,
        scratch_shapes=[pltpu.VMEM((512, BLK), F32)],
        compiler_params=pltpu.CompilerParams(vmem_limit_bytes=28 << 20),
        name="contract",
    )(incoming, pltpu.with_memory_space_constraint(blocks, pltpu.VMEM))
    gathered = lax.all_to_all(
        partial_value.reshape(128, 8, BLK), ("vp", "cd"), split_axis=0, concat_axis=0, tiled=True
    )
    return pl.pallas_call(
        collect_kernel,
        out_shape=jax.ShapeDtypeStruct((2, 2048), F32),
        in_specs=[VMEM, VMEM],
        out_specs=VMEM,
        compiler_params=pltpu.CompilerParams(vmem_limit_bytes=8 << 20),
        name="collect",
    )(spread, gathered)


def solution(mesh):
    return jax.shard_map(
        shards,
        mesh=mesh,
        in_specs=(P("vp", None), P(("vp", "cd"), None), P(), P(), P(), P(), P()),
        out_specs=P("vp", "cd"),
        check_vma=False,
    )
```

time: 43.8 us -> 42.7 us (0.975)
  Pallas kernels: 7.1 us -> 6.03 us
    pallas_call x1, Pallas kernels: 1.33 us -> 0.78 us  [shards(): pl.pallas_call(collect_kernel, out_shape=jax.ShapeDtypeStruct((2, 2048),...]
where the time goes in v3:
time: 42.7 us; the launch traced here: 42.4 us
  blocking collectives  36.3 us (85%)
  Pallas kernels  6.03 us (14%)
    all_to_all x1, blocking collectives, shards(): lax.all_to_all(partial_value.reshape(128, 8, BLK), ('vp', 'cd'), split_ax...  19.5 us
    all_to_all x1, blocking collectives, shards(): lax.all_to_all(outgoing.reshape(32, 16, BLK), 'vp', split_axis=0, concat_...  16.9 us
    pallas_call x1, Pallas kernels, shards(): pl.pallas_call(route_kernel, out_shape=(jax.ShapeDtypeStruct((512, BLK),...  4.21 us
    pallas_call x1, Pallas kernels, shards(): pl.pallas_call(contract_kernel, out_shape=jax.ShapeDtypeStruct((1024, BLK...  1.05 us

profile of v3, /device:TPU:1, one launch (start us, length us, event | category | flops | bytes accessed | tf_op | source)
XLA Modules:
  0.0 42.4 jit_solution(17798307093937824885)
XLA Ops:
  0.0 4.2 %route.1 = (bf16[512,128]{1,0:T(8,128)(2,1)S(1)}, bf16[1024,2048]{1,0:T(8,128)(2,1)S(1)}, f32[8,128]{1,0:T(8,128)S(1)}) custom-call(s32[200]{0:T(256)} %occ_h.1, s32[2,64]{1,0:T(2,128)} %bitcast.18, bf16[1024,128]{1,0:T(8,128)(2,1)} %bitcast.15, s32[1,512]{1,0:T(1,128)} %bitcast.16, s32[1,512]{1,0:T(1,128)} %bitcast.17, s32[1,64]{1,0:T(1,128)} %bitcast.19, ...), custom_call_target="tpu_custom_call" | custom-call | tf_op jit(solution)/shard_map/route/pallas_call | solution.py:148
  4.2 16.9 %all_to_all.10 = bf16[32,16,128]{2,1,0:T(8,128)(2,1)S(1)} all-to-all(bf16[32,16,128]{2,1,0:T(8,128)(2,1)S(1)} %bitcast.14), channel_id=1, replica_groups=mesh['vp'=32,'cd'=4] {'vp'}, dimensions={0} | all-to-all | bytes 262144 | tf_op jit(solution)/shard_map/all_to_all | solution.py:172
  21.1 1.0 %contract.1 = f32[1024,128]{1,0:T(8,128)S(1)} custom-call(bf16[512,128]{1,0:T(8,128)(2,1)S(1)} %bitcast.13, bf16[1024,2048]{1,0:T(8,128)(2,1)S(1)} %get-tuple-element.10.blocks), custom_call_target="tpu_custom_call" | custom-call | tf_op jit(solution)/shard_map/contract/pallas_call | solution.py:175
  22.1 19.5 %all_to_all.11.recv = f32[128,8,128]{2,1,0:T(8,128)S(1)} all-to-all(f32[128,8,128]{2,1,0:T(8,128)S(1)} %bitcast.12), channel_id=1, replica_groups=mesh['vp'=32,'cd'=4] {'vp','cd'}, dimensions={0} | all-to-all | bytes 1048576 | tf_op jit(solution)/shard_map/all_to_all | solution.py:184
  41.6 0.8 %collect.1 = f32[2,2048]{1,0:T(2,128)} custom-call(f32[8,128]{1,0:T(8,128)S(1)} %get-tuple-element.8.spread, f32[128,8,128]{2,1,0:T(8,128)S(1)} %all_to_all.11.recv), custom_call_target="tpu_custom_call" | custom-call | tf_op jit(solution)/shard_map/collect/pallas_call | solution.py:187

commit v4 on v3

--- a/solution.py
+++ b/solution.py
@@ -34,8 +34,8 @@
 
 
 def route_kernel(
-    occ_h, pair_h, amp_h, owner_h, cd_h, ab_h, integrals, out, blocks, spread,
-    occ, pair, amp, owner, cd, ab, lists_v, lists, sems, row_sems,
+    occ_h, pair_h, amp_h, owner_h, cd_h, ab_h, out, table, spread,
+    occ, pair, amp, owner, cd, ab, table_v, sems,
 ):
     copies = fetch(
         sems, (owner_h, owner), (cd_h, cd), (ab_h, ab), (occ_h, occ), (pair_h, pair), (amp_h, amp)
@@ -70,12 +70,14 @@
         spot = iota((nab, BLK), 1) == (source >> 4) * 4 + m
         value = jnp.where(spot, source.astype(F32), 0.0).astype(BF16)
         total = total + dot(ones_where(match & (order == float(m))), value)
-    lists_v[...] = total[:8].astype(jnp.int32)
-    to_scalars = pltpu.make_async_copy(lists_v, lists, sems.at[0])
+    slot = iota((8, 1), 0).astype(F32)
+    sector = jnp.sum(jnp.where(mine == slot, cdf, 0.0), axis=1, keepdims=True)
+    starts = jnp.zeros((8, BLK), F32)
+    for t in range(4):
+        starts = starts + jnp.where(sector == float(t), total[t:t + 1], 0.0)
+    table_v[...] = starts.astype(jnp.int32)
+    to_scalars = pltpu.make_async_copy(table_v, table, sems.at[0])
     to_scalars.start()
-    sector = [
-        jnp.sum(jnp.where(mine == float(s), cdf, 0.0)).astype(jnp.int32) for s in range(8)
-    ]
     hot32 = own == iota((32, nblk), 0) * 4 + y
     rank2 = dot(ones_where(hot32), before2)
     both = jnp.concatenate([own.astype(F32), cdf, jnp.zeros((14, nblk), F32)], axis=0)
@@ -85,15 +87,6 @@
     ids = (iota((32, 1), 0) * 4 + y).astype(F32)
     keep = (wide[:1] == ids) & (wide[1:2] == sym)
     code = jnp.where(keep, rank2 * 2.0 + parity.astype(F32), -1.0)
-    to_scalars.wait()
-    for s in range(8):
-        for cb in range(16):
-            start = pl.multiple_of(lists[sector[s], cb] * BLK, BLK)
-            pltpu.make_async_copy(
-                integrals.at[s * BLK:(s + 1) * BLK, pl.ds(start, BLK)],
-                blocks.at[s * BLK:(s + 1) * BLK, cb * BLK:(cb + 1) * BLK],
-                row_sems.at[s],
-            ).start()
     place = iota((32, 16, 2 * nblk), 1).astype(F32)
     select = ones_where(code[:, None, :] == place).reshape(512, 2 * nblk)
     shift = iota((nab, BLK), 0) == iota((nab, BLK), 1) + y * 16
@@ -101,12 +94,10 @@
     spread[...] = dot(ones_where(places), ones_where(shift))[8:]
     copies[5].wait()
     out[...] = dot(select, amp[...]).astype(BF16)
-    for s in range(8):
-        rows = blocks.at[s * BLK:(s + 1) * BLK, :]
-        pltpu.make_async_copy(rows, rows, row_sems.at[s]).wait()
-
-
-def contract_kernel(recv, blocks, out, wide):
+    to_scalars.wait()
+
+
+def contract_kernel(table, recv, integrals, out, wide):
     wide[...] = recv[...].astype(F32)
     slots = []
     for s in range(8):
@@ -114,7 +105,14 @@
         slots.append(jnp.concatenate(rows, axis=0).astype(BF16))
     a = jnp.concatenate(slots, axis=1)
     for pair_at in range(8):
-        result = dot(a, blocks[:, pair_at * 256:(pair_at + 1) * 256])
+        columns = []
+        for cb in (pair_at * 2, pair_at * 2 + 1):
+            parts = []
+            for s in range(8):
+                start = pl.multiple_of(table[s, cb] * BLK, BLK)
+                parts.append(integrals[s * BLK:(s + 1) * BLK, pl.ds(start, BLK)])
+            columns.append(jnp.concatenate(parts, axis=0))
+        result = dot(a, jnp.concatenate(columns, axis=1))
         for half in range(2):
             cb = pair_at * 2 + half
             for r in range(2):
@@ -133,6 +131,7 @@
 
 
 VMEM = pl.BlockSpec(memory_space=pltpu.VMEM)
+SMEM = pl.BlockSpec(memory_space=pltpu.SMEM)
 HBM = pl.BlockSpec(memory_space=pltpu.HBM)
 
 
@@ -145,15 +144,15 @@
     amp = amplitudes.reshape(2, nblk, BLK).transpose(1, 0, 2).reshape(2 * nblk, BLK)
     pair = pair_occ.T
     owner, cd, ab = block_owner.T, cd_sector[None, :], ab_sector[None, :]
-    outgoing, blocks, spread = pl.pallas_call(
+    outgoing, table, spread = pl.pallas_call(
         route_kernel,
         out_shape=(
             jax.ShapeDtypeStruct((512, BLK), BF16),
-            pltpu.VMEM((1024, 2048), BF16),
+            pltpu.SMEM((8, BLK), jnp.int32),
             jax.ShapeDtypeStruct((8, BLK), F32),
         ),
-        in_specs=[HBM] * 7,
-        out_specs=(VMEM, VMEM, VMEM),
+        in_specs=[HBM] * 6,
+        out_specs=(VMEM, SMEM, VMEM),
         scratch_shapes=[
             pltpu.SMEM(occ_irrep.shape, jnp.int32),
             pltpu.SMEM(pair.shape, jnp.int32),
@@ -162,25 +161,24 @@
             pltpu.VMEM(cd.shape, jnp.int32),
             pltpu.VMEM(ab.shape, jnp.int32),
             pltpu.VMEM((8, BLK), jnp.int32),
-            pltpu.SMEM((8, BLK), jnp.int32),
             pltpu.SemaphoreType.DMA((6,)),
-            pltpu.SemaphoreType.DMA((8,)),
         ],
         compiler_params=pltpu.CompilerParams(vmem_limit_bytes=16 << 20),
+        cost_estimate=pl.CostEstimate(flops=40 << 30, bytes_accessed=256 << 20, transcendentals=0),
         name="route",
-    )(*hbm(occ_irrep, pair, amp, owner, cd, ab, integrals))
+    )(*hbm(occ_irrep, pair, amp, owner, cd, ab))
     incoming = lax.all_to_all(
         outgoing.reshape(32, 16, BLK), "vp", split_axis=0, concat_axis=0, tiled=True
     ).reshape(512, BLK)
     partial_value = pl.pallas_call(
         contract_kernel,
         out_shape=jax.ShapeDtypeStruct((1024, BLK), F32),
-        in_specs=[VMEM, VMEM],
+        in_specs=[SMEM, VMEM, VMEM],
         out_specs=VMEM,
         scratch_shapes=[pltpu.VMEM((512, BLK), F32)],
         compiler_params=pltpu.CompilerParams(vmem_limit_bytes=28 << 20),
         name="contract",
-    )(incoming, pltpu.with_memory_space_constraint(blocks, pltpu.VMEM))
+    )(table, incoming, pltpu.with_memory_space_constraint(integrals, pltpu.VMEM))
     gathered = lax.all_to_all(
         partial_value.reshape(128, 8, BLK), ("vp", "cd"), split_axis=0, concat_axis=0, tiled=True
     )

time: 42.7 us -> 41.3 us (0.967)
  Pallas kernels: 6.03 us -> 4.59 us
    pallas_call x1, Pallas kernels: 4.21 us -> 2.23 us  [shards(): pl.pallas_call(route_kernel, out_shape=(jax.ShapeDtypeStruct((512, BLK),...]
    pallas_call x1, Pallas kernels: 1.05 us -> 1.58 us  [shards(): pl.pallas_call(contract_kernel, out_shape=jax.ShapeDtypeStruct((1024, BLK...]
where the time goes in v4:
time: 41.3 us; the launch traced here: 41.2 us
  blocking collectives  36.6 us (89%)
  Pallas kernels  4.59 us (11%)
    all_to_all x1, blocking collectives, shards(): lax.all_to_all(partial_value.reshape(128, 8, BLK), ('vp', 'cd'), split_ax...  19.5 us
    all_to_all x1, blocking collectives, shards(): lax.all_to_all(outgoing.reshape(32, 16, BLK), 'vp', split_axis=0, concat_...  17.1 us
    pallas_call x1, Pallas kernels, shards(): pl.pallas_call(route_kernel, out_shape=(jax.ShapeDtypeStruct((512, BLK),...  2.23 us
    pallas_call x1, Pallas kernels, shards(): pl.pallas_call(contract_kernel, out_shape=jax.ShapeDtypeStruct((1024, BLK...  1.58 us

profile of v4, /device:TPU:1, one launch (start us, length us, event | category | flops | bytes accessed | tf_op | source)
XLA Modules:
  0.0 41.2 jit_solution(15047819934698188397)
XLA Ops:
  0.0 0.0 copy-start
  0.0 2.2 %route.1 = (bf16[512,128]{1,0:T(8,128)(2,1)S(1)}, s32[8,128]{1,0:T(8,128)S(4)}, f32[8,128]{1,0:T(8,128)S(1)}) custom-call(s32[200]{0:T(256)} %occ_h.1, s32[2,64]{1,0:T(2,128)} %bitcast.18, bf16[1024,128]{1,0:T(8,128)(2,1)} %bitcast.15, s32[1,512]{1,0:T(1,128)} %bitcast.16, s32[1,512]{1,0:T(1,128)} %bitcast.17, s32[1,64]{1,0:T(1,128)} %bitcast.19), custom_call_target="tpu_custom_call" | custom-call | flops 42949672960 | bytes 268435456 | tf_op jit(solution)/shard_map/route/pallas_call | solution.py:147
  2.2 17.1 %all_to_all.10 = bf16[32,16,128]{2,1,0:T(8,128)(2,1)S(1)} all-to-all(bf16[32,16,128]{2,1,0:T(8,128)(2,1)S(1)} %bitcast.14), channel_id=1, replica_groups=mesh['vp'=32,'cd'=4] {'vp'}, dimensions={0} | all-to-all | bytes 262144 | tf_op jit(solution)/shard_map/all_to_all | solution.py:170
  19.4 0.0 copy-done
  19.4 1.6 %contract.1 = f32[1024,128]{1,0:T(8,128)S(1)} custom-call(s32[8,128]{1,0:T(8,128)S(4)} %get-tuple-element.9.table, bf16[512,128]{1,0:T(8,128)(2,1)S(1)} %bitcast.13, bf16[1024,8192]{1,0:T(8,128)(2,1)S(1)} %copy-done), custom_call_target="tpu_custom_call" | custom-call | tf_op jit(solution)/shard_map/contract/pallas_call | solution.py:173
  21.0 19.5 %all_to_all.11.recv = f32[128,8,128]{2,1,0:T(8,128)S(1)} all-to-all(f32[128,8,128]{2,1,0:T(8,128)S(1)} %bitcast.12), channel_id=1, replica_groups=mesh['vp'=32,'cd'=4] {'vp','cd'}, dimensions={0} | all-to-all | bytes 1048576 | tf_op jit(solution)/shard_map/all_to_all | solution.py:182
  40.4 0.8 %collect.1 = f32[2,2048]{1,0:T(2,128)} custom-call(f32[8,128]{1,0:T(8,128)S(1)} %get-tuple-element.8.spread, f32[128,8,128]{2,1,0:T(8,128)S(1)} %all_to_all.11.recv), custom_call_target="tpu_custom_call" | custom-call | tf_op jit(solution)/shard_map/collect/pallas_call | solution.py:185
Async XLA Ops:
  0.0 19.4 %copy-start = (bf16[1024,8192]{1,0:T(8,128)(2,1)S(1)}, bf16[1024,8192]{1,0:T(8,128)(2,1)}, u32[]{:S(2)}) copy-start(bf16[1024,8192]{1,0:T(8,128)(2,1)} %integrals.1) | copy-start | bytes 50331652

commit v5 on v4

--- a/solution.py
+++ b/solution.py
@@ -40,8 +40,8 @@
     copies = fetch(
         sems, (owner_h, owner), (cd_h, cd), (ab_h, ab), (occ_h, occ), (pair_h, pair), (amp_h, amp)
     )
-    vp = lax.axis_index("vp")
-    y = lax.axis_index("cd")
+    vp = (lax.axis_index("z") * 4 + lax.axis_index("x")) * 2 + lax.axis_index("c")
+    y = lax.axis_index("y")
     nblk = owner.shape[1]
     nab = ab.shape[1]
     half_col = iota((nblk, 2 * nblk), 1) >> 1
@@ -97,11 +97,16 @@
     to_scalars.wait()
 
 
-def contract_kernel(table, recv, integrals, out, wide):
+def contract_kernel(table, recv, integrals, own, other, wide):
+    core = lax.axis_index("c")
     wide[...] = recv[...].astype(F32)
     slots = []
     for s in range(8):
-        rows = [wide[pl.Slice(s * 2 + r, 32, stride=16), :] for r in range(2)]
+        rows = [
+            wide[pl.Slice(c * 16 + s * 2 + r, 16, stride=32), :]
+            for c in (core, 1 - core)
+            for r in range(2)
+        ]
         slots.append(jnp.concatenate(rows, axis=0).astype(BF16))
     a = jnp.concatenate(slots, axis=1)
     for pair_at in range(8):
@@ -115,10 +120,12 @@
         result = dot(a, jnp.concatenate(columns, axis=1))
         for half in range(2):
             cb = pair_at * 2 + half
-            for r in range(2):
-                out[pl.Slice((cb // 4) * 8 + r * 4 + cb % 4, 32, stride=32), :] = result[
-                    r * 32:(r + 1) * 32, half * BLK:(half + 1) * BLK
-                ]
+            for h, out in enumerate((own, other)):
+                for r in range(2):
+                    at = h * 32 + r * 16
+                    out[pl.Slice((cb // 4) * 8 + r * 4 + cb % 4, 16, stride=32), :] = result[
+                        at:at + 16, half * BLK:(half + 1) * BLK
+                    ]
 
 
 def collect_kernel(spread, recv, out):
@@ -168,19 +175,20 @@
         name="route",
     )(*hbm(occ_irrep, pair, amp, owner, cd, ab))
     incoming = lax.all_to_all(
-        outgoing.reshape(32, 16, BLK), "vp", split_axis=0, concat_axis=0, tiled=True
+        outgoing.reshape(32, 16, BLK), ("z", "x", "c"), split_axis=0, concat_axis=0, tiled=True
     ).reshape(512, BLK)
-    partial_value = pl.pallas_call(
+    own, other = pl.pallas_call(
         contract_kernel,
-        out_shape=jax.ShapeDtypeStruct((1024, BLK), F32),
+        out_shape=(jax.ShapeDtypeStruct((512, BLK), F32),) * 2,
         in_specs=[SMEM, VMEM, VMEM],
-        out_specs=VMEM,
+        out_specs=(VMEM, VMEM),
         scratch_shapes=[pltpu.VMEM((512, BLK), F32)],
         compiler_params=pltpu.CompilerParams(vmem_limit_bytes=28 << 20),
         name="contract",
     )(table, incoming, pltpu.with_memory_space_constraint(integrals, pltpu.VMEM))
+    chip_sum = own + lax.ppermute(other, "c", [(0, 1), (1, 0)])
     gathered = lax.all_to_all(
-        partial_value.reshape(128, 8, BLK), ("vp", "cd"), split_axis=0, concat_axis=0, tiled=True
+        chip_sum.reshape(64, 8, BLK), ("z", "x", "y"), split_axis=0, concat_axis=0, tiled=True
     )
     return pl.pallas_call(
         collect_kernel,
@@ -193,10 +201,12 @@
 
 
 def solution(mesh):
+    grid = jax.sharding.Mesh(mesh.devices.reshape(4, 4, 2, 4), ("z", "x", "c", "y"))
+    rows = ("z", "x", "c")
     return jax.shard_map(
         shards,
-        mesh=mesh,
-        in_specs=(P("vp", None), P(("vp", "cd"), None), P(), P(), P(), P(), P()),
-        out_specs=P("vp", "cd"),
+        mesh=grid,
+        in_specs=(P(rows, None), P(rows + ("y",), None), P(), P(), P(), P(), P()),
+        out_specs=P(rows, "y"),
         check_vma=False,
     )

time: 41.3 us -> 40.1 us (0.971)
  blocking collectives: 36.6 us -> 33.5 us
  waiting for transfers between devices: 0 us -> 1.16 us
  starting transfers between devices: 0 us -> 0.48 us
    all_to_all x2, blocking collectives: 36.6 us -> 33.5 us  [the longest x1 17.1 us: shards(): lax.all_to_all(outgoing.reshape(32, 16, BLK), ('z', 'x', 'c'), split_axis...]
    ppermute x0 -> x1, waiting for transfers between devices: none -> 1.16 us  [shards(): chip_sum = own + lax.ppermute(other, 'c', [(0, 1), (1, 0)])]
    ppermute x0 -> x1, starting transfers between devices: none -> 0.48 us  [shards(): chip_sum = own + lax.ppermute(other, 'c', [(0, 1), (1, 0)])]
  transfers between devices with their start and end apart: 0 -> 1, of which waited for: 0 -> 1; matrix products, arithmetic and copies ran while one was open for 0% -> 0% of each run, Pallas kernels for 0% -> 0%
where the time goes in v5:
time: 40.1 us; the launch traced here: 39.8 us
  blocking collectives  33.5 us (84%)
  Pallas kernels  4.64 us (12%)
  waiting for transfers between devices  1.16 us (3%)
  starting transfers between devices  0.48 us (1%)
    all_to_all x1, blocking collectives, shards(): lax.all_to_all(outgoing.reshape(32, 16, BLK), ('z', 'x', 'c'), split_axis...  17.1 us
    all_to_all x1, blocking collectives, shards(): lax.all_to_all(chip_sum.reshape(64, 8, BLK), ('z', 'x', 'y'), split_axis=...  16.3 us
    pallas_call x1, Pallas kernels, shards(): pl.pallas_call(route_kernel, out_shape=(jax.ShapeDtypeStruct((512, BLK),...  2.23 us
    pallas_call x1, Pallas kernels, shards(): pl.pallas_call(contract_kernel, out_shape=(jax.ShapeDtypeStruct((512, BLK...  1.7 us
    ppermute x1, waiting for transfers between devices, shards(): chip_sum = own + lax.ppermute(other, 'c', [(0, 1), (1, 0)])  1.16 us
  transfers between devices with their start and end apart: 1, of which 1 were waited for; matrix products, arithmetic and copies ran while one was open for 0% of the time, Pallas kernels for 0%

profile of v5, /device:TPU:1, one launch (start us, length us, event | category | flops | bytes accessed | tf_op | source)
XLA Modules:
  0.0 39.8 jit_solution(14306147122377635827)
XLA Ops:
  0.0 0.0 copy-start
  0.0 2.2 %route.1 = (bf16[512,128]{1,0:T(8,128)(2,1)S(1)}, s32[8,128]{1,0:T(8,128)S(4)}, f32[8,128]{1,0:T(8,128)S(1)}) custom-call(s32[200]{0:T(256)} %occ_h.1, s32[2,64]{1,0:T(2,128)} %bitcast.18, bf16[1024,128]{1,0:T(8,128)(2,1)} %bitcast.15, s32[1,512]{1,0:T(1,128)} %bitcast.16, s32[1,512]{1,0:T(1,128)} %bitcast.17, s32[1,64]{1,0:T(1,128)} %bitcast.19), custom_call_target="tpu_custom_call" | custom-call | flops 42949672960 | bytes 268435456 | tf_op jit(solution)/shard_map/route/pallas_call | solution.py:154
  2.2 17.1 %all_to_all.10 = bf16[32,16,128]{2,1,0:T(8,128)(2,1)S(1)} all-to-all(bf16[32,16,128]{2,1,0:T(8,128)(2,1)S(1)} %bitcast.14), channel_id=1, replica_groups=mesh['z'=4,'x'=4,'c'=2,'y'=4] {'z','x','c'}, dimensions={0} | all-to-all | bytes 262144 | tf_op jit(solution)/shard_map/all_to_all | solution.py:177
  19.4 0.0 copy-done
  19.4 1.7 %contract.1 = (f32[512,128]{1,0:T(8,128)S(1)}, f32[512,128]{1,0:T(8,128)S(1)}) custom-call(s32[8,128]{1,0:T(8,128)S(4)} %get-tuple-element.11.table, bf16[512,128]{1,0:T(8,128)(2,1)S(1)} %bitcast.13, bf16[1024,8192]{1,0:T(8,128)(2,1)S(1)} %copy-done), custom_call_target="tpu_custom_call" | custom-call | tf_op jit(solution)/shard_map/contract/pallas_call | solution.py:180
  21.1 0.5 %collective-permute-start = (f32[512,128]{1,0:T(8,128)S(1)}, f32[512,128]{1,0:T(8,128)S(1)}, u32[]{:S(2)}, u32[]{:S(2)}) collective-permute-start(f32[512,128]{1,0:T(8,128)S(1)} %get-tuple-element.14), channel_id=1, source_target_pairs={{0,4},{4,0},{1,5},{5,1},{2,6},{6,2},{3,7},{7,3},{8,12},{12,8},{9,1... | collective-permute-start | bytes 786440 | tf_op jit(solution)/shard_map/ppermute | solution.py:189
  21.6 1.2 %collective-permute-done = f32[512,128]{1,0:T(8,128)S(1)} collective-permute-done((f32[512,128]{1,0:T(8,128)S(1)}, f32[512,128]{1,0:T(8,128)S(1)}, u32[]{:S(2)}, u32[]{:S(2)}) %collective-permute-start) | collective-permute-done | bytes 262176 | tf_op jit(solution)/shard_map/ppermute | solution.py:189
  22.8 16.3 %all_to_all.11.recv = f32[64,8,128]{2,1,0:T(8,128)S(1)} all-to-all(f32[64,8,128]{2,1,0:T(8,128)S(1)} %add_bitcast_fusion), channel_id=1, replica_groups=mesh['z'=4,'x'=4,'c'=2,'y'=4] {'z','x','y'}, dimensions={0} | all-to-all | bytes 524288 | tf_op jit(solution)/shard_map/all_to_all | solution.py:190
  39.1 0.7 %collect.1 = f32[2,2048]{1,0:T(2,128)} custom-call(f32[8,128]{1,0:T(8,128)S(1)} %get-tuple-element.10.spread, f32[64,8,128]{2,1,0:T(8,128)S(1)} %all_to_all.11.recv), custom_call_target="tpu_custom_call" | custom-call | tf_op jit(solution)/shard_map/collect/pallas_call | solution.py:193
  (1 shorter events, 0.0 us)
Async XLA Ops:
  0.0 19.4 %copy-start = (bf16[1024,8192]{1,0:T(8,128)(2,1)S(1)}, bf16[1024,8192]{1,0:T(8,128)(2,1)}, u32[]{:S(2)}) copy-start(bf16[1024,8192]{1,0:T(8,128)(2,1)} %integrals.1) | copy-start | bytes 50331652
  21.1 1.6 %collective-permute-start = (f32[512,128]{1,0:T(8,128)S(1)}, f32[512,128]{1,0:T(8,128)S(1)}, u32[]{:S(2)}, u32[]{:S(2)}) collective-permute-start(f32[512,128]{1,0:T(8,128)S(1)} %get-tuple-element.14), channel_id=1, source_target_pairs={{0,4},{4,0},{1,5},{5,1},{2,6},{6,2},{3,7},{7,3},{8,12},{12,8},{9,1... | collective-permute-start | bytes 786440 | tf_op jit(solution)/shard_map/ppermute | solution.py:189

commit v6 on v5

--- a/solution.py
+++ b/solution.py
@@ -35,66 +35,58 @@
 
 def route_kernel(
     occ_h, pair_h, amp_h, owner_h, cd_h, ab_h, out, table, spread,
-    occ, pair, amp, owner, cd, ab, table_v, sems,
+    occ, pair, amp, owner, cd, ab, ab_s, wide, sems,
 ):
     copies = fetch(
-        sems, (owner_h, owner), (cd_h, cd), (ab_h, ab), (occ_h, occ), (pair_h, pair), (amp_h, amp)
+        sems, (owner_h, owner), (cd_h, cd), (ab_h, ab), (ab_h, ab_s), (occ_h, occ), (pair_h, pair), (amp_h, amp)
     )
     vp = (lax.axis_index("z") * 4 + lax.axis_index("x")) * 2 + lax.axis_index("c")
     y = lax.axis_index("y")
     nblk = owner.shape[1]
     nab = ab.shape[1]
-    half_col = iota((nblk, 2 * nblk), 1) >> 1
     before = ones_where(iota((nblk, nblk), 0) < iota((nblk, nblk), 1))
-    before2 = ones_where(iota((nblk, 2 * nblk), 0) < half_col)
-    widen = ones_where(iota((nblk, 2 * nblk), 0) == half_col)
     j0 = iota((nab, nab), 0)
     j1 = iota((nab, nab), 1)
     within = ones_where((j0 < j1) & ((j0 >> 4) == (j1 >> 4)))
-    for copy in copies[:5]:
+    for copy in copies[:6]:
         copy.wait()
-    own = owner[...]
-    cdf = cd[...].astype(F32)
-    hot = own == vp * 4 + y
-    rank = dot(jnp.broadcast_to(ones_where(hot), (16, nblk)), before)[:1]
-    mine = jnp.where(hot, rank, -1.0)
     sym0 = row_symmetry(occ, pair, 2 * vp)
     sym1 = row_symmetry(occ, pair, 2 * vp + 1)
+    cdrow = cd[...]
+    cdf = cdrow.astype(F32)
+    prow = iota((48, 1), 0)
+    hot = owner[...] == jnp.where(prow < 32, prow, vp) * 4 + y
+    rank = dot(ones_where(hot), before)
+    for panel in range(nab // 16):
+        seen = jnp.int32(0)
+        for j in range(panel * 16, panel * 16 + 16):
+            t = ab_s[0, j]
+            table[t, panel * 4 + ((seen >> (t * 8)) & 255)] = jnp.int32(j)
+            seen = seen + (jnp.int32(1) << (t * 8))
     row = iota((16, 1), 0)
     wanted = jnp.where(row < 8, row, jnp.where(row < 12, sym0, sym1))
     match = ab[...] == wanted
     order = dot(ones_where(match), within)
-    source = iota((nab, BLK), 0)
-    total = jnp.zeros((16, BLK), F32)
-    for m in range(4):
-        spot = iota((nab, BLK), 1) == (source >> 4) * 4 + m
-        value = jnp.where(spot, source.astype(F32), 0.0).astype(BF16)
-        total = total + dot(ones_where(match & (order == float(m))), value)
-    slot = iota((8, 1), 0).astype(F32)
-    sector = jnp.sum(jnp.where(mine == slot, cdf, 0.0), axis=1, keepdims=True)
-    starts = jnp.zeros((8, BLK), F32)
-    for t in range(4):
-        starts = starts + jnp.where(sector == float(t), total[t:t + 1], 0.0)
-    table_v[...] = starts.astype(jnp.int32)
-    to_scalars = pltpu.make_async_copy(table_v, table, sems.at[0])
-    to_scalars.start()
-    hot32 = own == iota((32, nblk), 0) * 4 + y
-    rank2 = dot(ones_where(hot32), before2)
-    both = jnp.concatenate([own.astype(F32), cdf, jnp.zeros((14, nblk), F32)], axis=0)
-    wide = dot(both.astype(BF16), widen)
-    parity = iota((1, 2 * nblk), 1) & 1
-    sym = jnp.where(parity == 0, sym0, sym1).astype(F32)
-    ids = (iota((32, 1), 0) * 4 + y).astype(F32)
-    keep = (wide[:1] == ids) & (wide[1:2] == sym)
-    code = jnp.where(keep, rank2 * 2.0 + parity.astype(F32), -1.0)
-    place = iota((32, 16, 2 * nblk), 1).astype(F32)
-    select = ones_where(code[:, None, :] == place).reshape(512, 2 * nblk)
+    mine = jnp.where(hot[32:33], rank[32:33], -1.0)
+    for s in range(8):
+        sector = jnp.sum(jnp.where(mine == float(s), cdf, 0.0))
+        table[4, s] = sector.astype(jnp.int32)
+    place = iota((32, 8, nblk), 1).astype(F32)
+    parts = []
+    for r, sym in enumerate((sym0, sym1)):
+        code = jnp.where(hot[:32] & (cdrow == sym), rank[:32], -1.0)
+        select = ones_where(code[:, None, :] == place).reshape(256, nblk)
+        parts.append(select)
+    copies[-1].wait()
+    wide[...] = amp[...].astype(F32)
+    sums = [
+        dot(parts[r], wide[pl.Slice(r, nblk, stride=2), :].astype(BF16)).reshape(32, 8, BLK)
+        for r in range(2)
+    ]
+    out[...] = jnp.concatenate(sums, axis=1).reshape(512, BLK).astype(BF16)
     shift = iota((nab, BLK), 0) == iota((nab, BLK), 1) + y * 16
     places = match & (order == (row & 3).astype(F32))
     spread[...] = dot(ones_where(places), ones_where(shift))[8:]
-    copies[5].wait()
-    out[...] = dot(select, amp[...]).astype(BF16)
-    to_scalars.wait()
 
 
 def contract_kernel(table, recv, integrals, own, other, wide):
@@ -103,28 +95,35 @@
     slots = []
     for s in range(8):
         rows = [
-            wide[pl.Slice(c * 16 + s * 2 + r, 16, stride=32), :]
+            wide[pl.Slice(c * 16 + r * 8 + s, 16, stride=32), :]
             for c in (core, 1 - core)
             for r in range(2)
         ]
         slots.append(jnp.concatenate(rows, axis=0).astype(BF16))
     a = jnp.concatenate(slots, axis=1)
-    for pair_at in range(8):
-        columns = []
-        for cb in (pair_at * 2, pair_at * 2 + 1):
-            parts = []
-            for s in range(8):
-                start = pl.multiple_of(table[s, cb] * BLK, BLK)
-                parts.append(integrals[s * BLK:(s + 1) * BLK, pl.ds(start, BLK)])
-            columns.append(jnp.concatenate(parts, axis=0))
-        result = dot(a, jnp.concatenate(columns, axis=1))
-        for half in range(2):
-            cb = pair_at * 2 + half
+    rows = [table[4, s] for s in range(8)]
+
+    def block(s, cb):
+        start = pl.multiple_of(table[rows[s], cb] * BLK, BLK)
+        return integrals[s * BLK:(s + 1) * BLK, pl.ds(start, BLK)]
+
+    for panels in range(2):
+        result = jnp.zeros((64, 8 * BLK), F32)
+        for s in range(0, 8, 2):
+            weights = [
+                jnp.concatenate([block(t, panels * 8 + i) for i in range(8)], axis=1)
+                for t in (s, s + 1)
+            ]
+            result = result + dot(
+                a[:, s * BLK:(s + 2) * BLK], jnp.concatenate(weights, axis=0)
+            )
+        for i in range(8):
+            cb = panels * 8 + i
             for h, out in enumerate((own, other)):
                 for r in range(2):
                     at = h * 32 + r * 16
                     out[pl.Slice((cb // 4) * 8 + r * 4 + cb % 4, 16, stride=32), :] = result[
-                        at:at + 16, half * BLK:(half + 1) * BLK
+                        at:at + 16, i * BLK:(i + 1) * BLK
                     ]
 
 
@@ -167,8 +166,9 @@
             pltpu.VMEM(owner.shape, jnp.int32),
             pltpu.VMEM(cd.shape, jnp.int32),
             pltpu.VMEM(ab.shape, jnp.int32),
-            pltpu.VMEM((8, BLK), jnp.int32),
-            pltpu.SemaphoreType.DMA((6,)),
+            pltpu.SMEM(ab.shape, jnp.int32),
+            pltpu.VMEM(amp.shape, F32),
+            pltpu.SemaphoreType.DMA((7,)),
         ],
         compiler_params=pltpu.CompilerParams(vmem_limit_bytes=16 << 20),
         cost_estimate=pl.CostEstimate(flops=40 << 30, bytes_accessed=256 << 20, transcendentals=0),

time: 40.1 us -> 39.5 us (0.985)
  Pallas kernels: 4.64 us -> 4.04 us
    pallas_call x1, Pallas kernels: 2.23 us -> 1.76 us  [shards(): pl.pallas_call(route_kernel, out_shape=(jax.ShapeDtypeStruct((512, BLK),...]
where the time goes in v6:
time: 39.5 us; the launch traced here: 39.2 us
  blocking collectives  33.5 us (85%)
  Pallas kernels  4.04 us (10%)
  waiting for transfers between devices  1.16 us (3%)
  starting transfers between devices  0.48 us (1%)
    all_to_all x1, blocking collectives, shards(): lax.all_to_all(outgoing.reshape(32, 16, BLK), ('z', 'x', 'c'), split_axis...  17.1 us
    all_to_all x1, blocking collectives, shards(): lax.all_to_all(chip_sum.reshape(64, 8, BLK), ('z', 'x', 'y'), split_axis=...  16.3 us
    pallas_call x1, Pallas kernels, shards(): pl.pallas_call(route_kernel, out_shape=(jax.ShapeDtypeStruct((512, BLK),...  1.76 us
    pallas_call x1, Pallas kernels, shards(): pl.pallas_call(contract_kernel, out_shape=(jax.ShapeDtypeStruct((512, BLK...  1.57 us
    ppermute x1, waiting for transfers between devices, shards(): chip_sum = own + lax.ppermute(other, 'c', [(0, 1), (1, 0)])  1.16 us
  transfers between devices with their start and end apart: 1, of which 1 were waited for; matrix products, arithmetic and copies ran while one was open for 0% of the time, Pallas kernels for 0%

profile of v6, /device:TPU:1, one launch (start us, length us, event | category | flops | bytes accessed | tf_op | source)
XLA Modules:
  0.0 39.2 jit_solution(1300744729310426404)
XLA Ops:
  0.0 0.0 copy-start
  0.0 1.8 %route.1 = (bf16[512,128]{1,0:T(8,128)(2,1)S(1)}, s32[8,128]{1,0:T(8,128)S(4)}, f32[8,128]{1,0:T(8,128)S(1)}) custom-call(s32[200]{0:T(256)} %occ_h.1, s32[2,64]{1,0:T(2,128)} %bitcast.18, bf16[1024,128]{1,0:T(8,128)(2,1)} %bitcast.15, s32[1,512]{1,0:T(1,128)} %bitcast.16, s32[1,512]{1,0:T(1,128)} %bitcast.17, s32[1,64]{1,0:T(1,128)} %bitcast.19), custom_call_target="tpu_custom_call" | custom-call | flops 42949672960 | bytes 268435456 | tf_op jit(solution)/shard_map/route/pallas_call | solution.py:153
  1.8 17.1 %all_to_all.10 = bf16[32,16,128]{2,1,0:T(8,128)(2,1)S(1)} all-to-all(bf16[32,16,128]{2,1,0:T(8,128)(2,1)S(1)} %bitcast.14), channel_id=1, replica_groups=mesh['z'=4,'x'=4,'c'=2,'y'=4] {'z','x','c'}, dimensions={0} | all-to-all | bytes 262144 | tf_op jit(solution)/shard_map/all_to_all | solution.py:177
  18.9 0.0 copy-done
  18.9 1.6 %contract.1 = (f32[512,128]{1,0:T(8,128)S(1)}, f32[512,128]{1,0:T(8,128)S(1)}) custom-call(s32[8,128]{1,0:T(8,128)S(4)} %get-tuple-element.11.table, bf16[512,128]{1,0:T(8,128)(2,1)S(1)} %bitcast.13, bf16[1024,8192]{1,0:T(8,128)(2,1)S(1)} %copy-done), custom_call_target="tpu_custom_call" | custom-call | tf_op jit(solution)/shard_map/contract/pallas_call | solution.py:180
  20.5 0.5 %collective-permute-start = (f32[512,128]{1,0:T(8,128)S(1)}, f32[512,128]{1,0:T(8,128)S(1)}, u32[]{:S(2)}, u32[]{:S(2)}) collective-permute-start(f32[512,128]{1,0:T(8,128)S(1)} %get-tuple-element.14), channel_id=1, source_target_pairs={{0,4},{4,0},{1,5},{5,1},{2,6},{6,2},{3,7},{7,3},{8,12},{12,8},{9,1... | collective-permute-start | bytes 786440 | tf_op jit(solution)/shard_map/ppermute | solution.py:189
  21.0 1.2 %collective-permute-done = f32[512,128]{1,0:T(8,128)S(1)} collective-permute-done((f32[512,128]{1,0:T(8,128)S(1)}, f32[512,128]{1,0:T(8,128)S(1)}, u32[]{:S(2)}, u32[]{:S(2)}) %collective-permute-start) | collective-permute-done | bytes 262176 | tf_op jit(solution)/shard_map/ppermute | solution.py:189
  22.2 16.3 %all_to_all.11.recv = f32[64,8,128]{2,1,0:T(8,128)S(1)} all-to-all(f32[64,8,128]{2,1,0:T(8,128)S(1)} %add_bitcast_fusion), channel_id=1, replica_groups=mesh['z'=4,'x'=4,'c'=2,'y'=4] {'z','x','y'}, dimensions={0} | all-to-all | bytes 524288 | tf_op jit(solution)/shard_map/all_to_all | solution.py:190
  38.5 0.7 %collect.1 = f32[2,2048]{1,0:T(2,128)} custom-call(f32[8,128]{1,0:T(8,128)S(1)} %get-tuple-element.10.spread, f32[64,8,128]{2,1,0:T(8,128)S(1)} %all_to_all.11.recv), custom_call_target="tpu_custom_call" | custom-call | tf_op jit(solution)/shard_map/collect/pallas_call | solution.py:193
  (1 shorter events, 0.0 us)
Async XLA Ops:
  0.0 18.9 %copy-start = (bf16[1024,8192]{1,0:T(8,128)(2,1)S(1)}, bf16[1024,8192]{1,0:T(8,128)(2,1)}, u32[]{:S(2)}) copy-start(bf16[1024,8192]{1,0:T(8,128)(2,1)} %integrals.1) | copy-start | bytes 50331652
  20.5 1.6 %collective-permute-start = (f32[512,128]{1,0:T(8,128)S(1)}, f32[512,128]{1,0:T(8,128)S(1)}, u32[]{:S(2)}, u32[]{:S(2)}) collective-permute-start(f32[512,128]{1,0:T(8,128)S(1)} %get-tuple-element.14), channel_id=1, source_target_pairs={{0,4},{4,0},{1,5},{5,1},{2,6},{6,2},{3,7},{7,3},{8,12},{12,8},{9,1... | collective-permute-start | bytes 786440 | tf_op jit(solution)/shard_map/ppermute | solution.py:189

commit v7 on v6

--- a/solution.py
+++ b/solution.py
@@ -55,7 +55,7 @@
     cdrow = cd[...]
     cdf = cdrow.astype(F32)
     prow = iota((48, 1), 0)
-    hot = owner[...] == jnp.where(prow < 32, prow, vp) * 4 + y
+    hot = owner[...] == jnp.where(prow < 32, (prow & 15) * 2 + (prow >> 4), vp) * 4 + y
     rank = dot(ones_where(hot), before)
     for panel in range(nab // 16):
         seen = jnp.int32(0)
@@ -91,11 +91,12 @@
 
 def contract_kernel(table, recv, integrals, own, other, wide):
     core = lax.axis_index("c")
-    wide[...] = recv[...].astype(F32)
+    for q in range(32):
+        wide[q * 17:q * 17 + 16, :] = recv[q * 16:q * 16 + 16, :].astype(F32)
     slots = []
     for s in range(8):
         rows = [
-            wide[pl.Slice(c * 16 + r * 8 + s, 16, stride=32), :]
+            wide[pl.Slice(c * 272 + r * 8 + s, 16, stride=17), :]
             for c in (core, 1 - core)
             for r in range(2)
         ]
@@ -122,7 +123,7 @@
             for h, out in enumerate((own, other)):
                 for r in range(2):
                     at = h * 32 + r * 16
-                    out[pl.Slice((cb // 4) * 8 + r * 4 + cb % 4, 16, stride=32), :] = result[
+                    out[pl.Slice((cb // 4) * 128 + r * 4 + cb % 4, 16, stride=8), :] = result[
                         at:at + 16, i * BLK:(i + 1) * BLK
                     ]
 
@@ -175,20 +176,20 @@
         name="route",
     )(*hbm(occ_irrep, pair, amp, owner, cd, ab))
     incoming = lax.all_to_all(
-        outgoing.reshape(32, 16, BLK), ("z", "x", "c"), split_axis=0, concat_axis=0, tiled=True
+        outgoing.reshape(32, 16, BLK), ("c", "z", "x"), split_axis=0, concat_axis=0, tiled=True
     ).reshape(512, BLK)
     own, other = pl.pallas_call(
         contract_kernel,
         out_shape=(jax.ShapeDtypeStruct((512, BLK), F32),) * 2,
         in_specs=[SMEM, VMEM, VMEM],
         out_specs=(VMEM, VMEM),
-        scratch_shapes=[pltpu.VMEM((512, BLK), F32)],
+        scratch_shapes=[pltpu.VMEM((544, BLK), F32)],
         compiler_params=pltpu.CompilerParams(vmem_limit_bytes=28 << 20),
         name="contract",
     )(table, incoming, pltpu.with_memory_space_constraint(integrals, pltpu.VMEM))
     chip_sum = own + lax.ppermute(other, "c", [(0, 1), (1, 0)])
     gathered = lax.all_to_all(
-        chip_sum.reshape(64, 8, BLK), ("z", "x", "y"), split_axis=0, concat_axis=0, tiled=True
+        chip_sum.reshape(64, 8, BLK), ("y", "z", "x"), split_axis=0, concat_axis=0, tiled=True
     )
     return pl.pallas_call(
         collect_kernel,

time: 39.5 us -> 39.4 us (level)
  no operation moved by 1% of the time
where the time goes in v7:
time: 39.4 us; the launch traced here: 39.1 us
  blocking collectives  33.4 us (85%)
  Pallas kernels  3.87 us (10%)
  waiting for transfers between devices  1.16 us (3%)
  starting transfers between devices  0.61 us (2%)
    all_to_all x1, blocking collectives, shards(): lax.all_to_all(outgoing.reshape(32, 16, BLK), ('c', 'z', 'x'), split_axis...  17 us
    all_to_all x1, blocking collectives, shards(): lax.all_to_all(chip_sum.reshape(64, 8, BLK), ('y', 'z', 'x'), split_axis=...  16.3 us
    pallas_call x1, Pallas kernels, shards(): pl.pallas_call(route_kernel, out_shape=(jax.ShapeDtypeStruct((512, BLK),...  1.76 us
    pallas_call x1, Pallas kernels, shards(): pl.pallas_call(contract_kernel, out_shape=(jax.ShapeDtypeStruct((512, BLK...  1.4 us
    ppermute x1, waiting for transfers between devices, shards(): chip_sum = own + lax.ppermute(other, 'c', [(0, 1), (1, 0)])  1.16 us
  transfers between devices with their start and end apart: 1, of which 1 were waited for; matrix products, arithmetic and copies ran while one was open for 0% of the time, Pallas kernels for 0%

profile of v7, /device:TPU:1, one launch (start us, length us, event | category | flops | bytes accessed | tf_op | source)
XLA Modules:
  0.0 39.1 jit_solution(10254952391221191830)
XLA Ops:
  0.0 0.0 copy-start
  0.0 1.8 %route.1 = (bf16[512,128]{1,0:T(8,128)(2,1)S(1)}, s32[8,128]{1,0:T(8,128)S(4)}, f32[8,128]{1,0:T(8,128)S(1)}) custom-call(s32[200]{0:T(256)} %occ_h.1, s32[2,64]{1,0:T(2,128)} %bitcast.18, bf16[1024,128]{1,0:T(8,128)(2,1)} %bitcast.15, s32[1,512]{1,0:T(1,128)} %bitcast.16, s32[1,512]{1,0:T(1,128)} %bitcast.17, s32[1,64]{1,0:T(1,128)} %bitcast.19), custom_call_target="tpu_custom_call" | custom-call | flops 42949672960 | bytes 268435456 | tf_op jit(solution)/shard_map/route/pallas_call | solution.py:154
  1.8 17.0 %all_to_all.10 = bf16[32,16,128]{2,1,0:T(8,128)(2,1)S(1)} all-to-all(bf16[32,16,128]{2,1,0:T(8,128)(2,1)S(1)} %bitcast.14), channel_id=1, replica_groups=mesh['z'=4,'x'=4,'c'=2,'y'=4] {'c','z','x'}, dimensions={0} | all-to-all | bytes 262144 | tf_op jit(solution)/shard_map/all_to_all | solution.py:178
  18.8 0.0 copy-done
  18.8 1.4 %contract.1 = (f32[512,128]{1,0:T(8,128)S(1)}, f32[512,128]{1,0:T(8,128)S(1)}) custom-call(s32[8,128]{1,0:T(8,128)S(4)} %get-tuple-element.11.table, bf16[512,128]{1,0:T(8,128)(2,1)S(1)} %bitcast.13, bf16[1024,8192]{1,0:T(8,128)(2,1)S(1)} %copy-done), custom_call_target="tpu_custom_call" | custom-call | tf_op jit(solution)/shard_map/contract/pallas_call | solution.py:181
  20.2 0.6 %collective-permute-start = (f32[512,128]{1,0:T(8,128)S(1)}, f32[512,128]{1,0:T(8,128)S(1)}, u32[]{:S(2)}, u32[]{:S(2)}) collective-permute-start(f32[512,128]{1,0:T(8,128)S(1)} %get-tuple-element.14), channel_id=1, source_target_pairs={{0,4},{4,0},{1,5},{5,1},{2,6},{6,2},{3,7},{7,3},{8,12},{12,8},{9,1... | collective-permute-start | bytes 786440 | tf_op jit(solution)/shard_map/ppermute | solution.py:190
  20.8 1.2 %collective-permute-done = f32[512,128]{1,0:T(8,128)S(1)} collective-permute-done((f32[512,128]{1,0:T(8,128)S(1)}, f32[512,128]{1,0:T(8,128)S(1)}, u32[]{:S(2)}, u32[]{:S(2)}) %collective-permute-start) | collective-permute-done | bytes 262176 | tf_op jit(solution)/shard_map/ppermute | solution.py:190
  22.0 16.3 %all_to_all.11.recv = f32[64,8,128]{2,1,0:T(8,128)S(1)} all-to-all(f32[64,8,128]{2,1,0:T(8,128)S(1)} %add_bitcast_fusion), channel_id=1, replica_groups=mesh['z'=4,'x'=4,'c'=2,'y'=4] {'y','z','x'}, dimensions={0} | all-to-all | bytes 524288 | tf_op jit(solution)/shard_map/all_to_all | solution.py:191
  38.4 0.7 %collect.1 = f32[2,2048]{1,0:T(2,128)} custom-call(f32[8,128]{1,0:T(8,128)S(1)} %get-tuple-element.10.spread, f32[64,8,128]{2,1,0:T(8,128)S(1)} %all_to_all.11.recv), custom_call_target="tpu_custom_call" | custom-call | tf_op jit(solution)/shard_map/collect/pallas_call | solution.py:194
  (1 shorter events, 0.0 us)
Async XLA Ops:
  0.0 18.8 %copy-start = (bf16[1024,8192]{1,0:T(8,128)(2,1)S(1)}, bf16[1024,8192]{1,0:T(8,128)(2,1)}, u32[]{:S(2)}) copy-start(bf16[1024,8192]{1,0:T(8,128)(2,1)} %integrals.1) | copy-start | bytes 50331652
  20.2 1.8 %collective-permute-start = (f32[512,128]{1,0:T(8,128)S(1)}, f32[512,128]{1,0:T(8,128)S(1)}, u32[]{:S(2)}, u32[]{:S(2)}) collective-permute-start(f32[512,128]{1,0:T(8,128)S(1)} %get-tuple-element.14), channel_id=1, source_target_pairs={{0,4},{4,0},{1,5},{5,1},{2,6},{6,2},{3,7},{7,3},{8,12},{12,8},{9,1... | collective-permute-start | bytes 786440 | tf_op jit(solution)/shard_map/ppermute | solution.py:190

commit v8 on v7

--- a/solution.py
+++ b/solution.py
@@ -57,20 +57,10 @@
     prow = iota((48, 1), 0)
     hot = owner[...] == jnp.where(prow < 32, (prow & 15) * 2 + (prow >> 4), vp) * 4 + y
     rank = dot(ones_where(hot), before)
-    for panel in range(nab // 16):
-        seen = jnp.int32(0)
-        for j in range(panel * 16, panel * 16 + 16):
-            t = ab_s[0, j]
-            table[t, panel * 4 + ((seen >> (t * 8)) & 255)] = jnp.int32(j)
-            seen = seen + (jnp.int32(1) << (t * 8))
     row = iota((16, 1), 0)
     wanted = jnp.where(row < 8, row, jnp.where(row < 12, sym0, sym1))
     match = ab[...] == wanted
     order = dot(ones_where(match), within)
-    mine = jnp.where(hot[32:33], rank[32:33], -1.0)
-    for s in range(8):
-        sector = jnp.sum(jnp.where(mine == float(s), cdf, 0.0))
-        table[4, s] = sector.astype(jnp.int32)
     place = iota((32, 8, nblk), 1).astype(F32)
     parts = []
     for r, sym in enumerate((sym0, sym1)):
@@ -84,6 +74,16 @@
         for r in range(2)
     ]
     out[...] = jnp.concatenate(sums, axis=1).reshape(512, BLK).astype(BF16)
+    mine = jnp.where(hot[32:33], rank[32:33], -1.0)
+    for s in range(8):
+        sector = jnp.sum(jnp.where(mine == float(s), cdf, 0.0))
+        table[4, s] = sector.astype(jnp.int32)
+    for panel in range(nab // 16):
+        seen = jnp.int32(0)
+        for j in range(panel * 16, panel * 16 + 16):
+            t = ab_s[0, j]
+            table[t, panel * 4 + ((seen >> (t * 8)) & 255)] = jnp.int32(j)
+            seen = seen + (jnp.int32(1) << (t * 8))
     shift = iota((nab, BLK), 0) == iota((nab, BLK), 1) + y * 16
     places = match & (order == (row & 3).astype(F32))
     spread[...] = dot(ones_where(places), ones_where(shift))[8:]

time: 39.4 us -> 39.3 us (level)
  no operation moved by 1% of the time
where the time goes in v8:
time: 39.3 us; the launch traced here: 39 us
  blocking collectives  33.4 us (85%)
  Pallas kernels  3.8 us (10%)
  waiting for transfers between devices  1.16 us (3%)
  starting transfers between devices  0.61 us (2%)
    all_to_all x1, blocking collectives, shards(): lax.all_to_all(outgoing.reshape(32, 16, BLK), ('c', 'z', 'x'), split_axis...  17 us
    all_to_all x1, blocking collectives, shards(): lax.all_to_all(chip_sum.reshape(64, 8, BLK), ('y', 'z', 'x'), split_axis=...  16.3 us
    pallas_call x1, Pallas kernels, shards(): pl.pallas_call(route_kernel, out_shape=(jax.ShapeDtypeStruct((512, BLK),...  1.68 us
    pallas_call x1, Pallas kernels, shards(): pl.pallas_call(contract_kernel, out_shape=(jax.ShapeDtypeStruct((512, BLK...  1.4 us
    ppermute x1, waiting for transfers between devices, shards(): chip_sum = own + lax.ppermute(other, 'c', [(0, 1), (1, 0)])  1.16 us
  transfers between devices with their start and end apart: 1, of which 1 were waited for; matrix products, arithmetic and copies ran while one was open for 0% of the time, Pallas kernels for 0%

profile of v8, /device:TPU:1, one launch (start us, length us, event | category | flops | bytes accessed | tf_op | source)
XLA Modules:
  0.0 39.0 jit_solution(11085311792318268958)
XLA Ops:
  0.0 0.0 copy-start
  0.0 1.7 %route.1 = (bf16[512,128]{1,0:T(8,128)(2,1)S(1)}, s32[8,128]{1,0:T(8,128)S(4)}, f32[8,128]{1,0:T(8,128)S(1)}) custom-call(s32[200]{0:T(256)} %occ_h.1, s32[2,64]{1,0:T(2,128)} %bitcast.18, bf16[1024,128]{1,0:T(8,128)(2,1)} %bitcast.15, s32[1,512]{1,0:T(1,128)} %bitcast.16, s32[1,512]{1,0:T(1,128)} %bitcast.17, s32[1,64]{1,0:T(1,128)} %bitcast.19), custom_call_target="tpu_custom_call" | custom-call | flops 42949672960 | bytes 268435456 | tf_op jit(solution)/shard_map/route/pallas_call | solution.py:154
  1.7 17.0 %all_to_all.10 = bf16[32,16,128]{2,1,0:T(8,128)(2,1)S(1)} all-to-all(bf16[32,16,128]{2,1,0:T(8,128)(2,1)S(1)} %bitcast.14), channel_id=1, replica_groups=mesh['z'=4,'x'=4,'c'=2,'y'=4] {'c','z','x'}, dimensions={0} | all-to-all | bytes 262144 | tf_op jit(solution)/shard_map/all_to_all | solution.py:178
  18.7 0.0 copy-done
  18.7 1.4 %contract.1 = (f32[512,128]{1,0:T(8,128)S(1)}, f32[512,128]{1,0:T(8,128)S(1)}) custom-call(s32[8,128]{1,0:T(8,128)S(4)} %get-tuple-element.11.table, bf16[512,128]{1,0:T(8,128)(2,1)S(1)} %bitcast.13, bf16[1024,8192]{1,0:T(8,128)(2,1)S(1)} %copy-done), custom_call_target="tpu_custom_call" | custom-call | tf_op jit(solution)/shard_map/contract/pallas_call | solution.py:181
  20.1 0.6 %collective-permute-start = (f32[512,128]{1,0:T(8,128)S(1)}, f32[512,128]{1,0:T(8,128)S(1)}, u32[]{:S(2)}, u32[]{:S(2)}) collective-permute-start(f32[512,128]{1,0:T(8,128)S(1)} %get-tuple-element.14), channel_id=1, source_target_pairs={{0,4},{4,0},{1,5},{5,1},{2,6},{6,2},{3,7},{7,3},{8,12},{12,8},{9,1... | collective-permute-start | bytes 786440 | tf_op jit(solution)/shard_map/ppermute | solution.py:190
  20.7 1.2 %collective-permute-done = f32[512,128]{1,0:T(8,128)S(1)} collective-permute-done((f32[512,128]{1,0:T(8,128)S(1)}, f32[512,128]{1,0:T(8,128)S(1)}, u32[]{:S(2)}, u32[]{:S(2)}) %collective-permute-start) | collective-permute-done | bytes 262176 | tf_op jit(solution)/shard_map/ppermute | solution.py:190
  21.9 16.3 %all_to_all.11.recv = f32[64,8,128]{2,1,0:T(8,128)S(1)} all-to-all(f32[64,8,128]{2,1,0:T(8,128)S(1)} %add_bitcast_fusion), channel_id=1, replica_groups=mesh['z'=4,'x'=4,'c'=2,'y'=4] {'y','z','x'}, dimensions={0} | all-to-all | bytes 524288 | tf_op jit(solution)/shard_map/all_to_all | solution.py:191
  38.3 0.7 %collect.1 = f32[2,2048]{1,0:T(2,128)} custom-call(f32[8,128]{1,0:T(8,128)S(1)} %get-tuple-element.10.spread, f32[64,8,128]{2,1,0:T(8,128)S(1)} %all_to_all.11.recv), custom_call_target="tpu_custom_call" | custom-call | tf_op jit(solution)/shard_map/collect/pallas_call | solution.py:194
  (1 shorter events, 0.0 us)
Async XLA Ops:
  0.0 18.7 %copy-start = (bf16[1024,8192]{1,0:T(8,128)(2,1)S(1)}, bf16[1024,8192]{1,0:T(8,128)(2,1)}, u32[]{:S(2)}) copy-start(bf16[1024,8192]{1,0:T(8,128)(2,1)} %integrals.1) | copy-start | bytes 50331652
  20.1 1.8 %collective-permute-start = (f32[512,128]{1,0:T(8,128)S(1)}, f32[512,128]{1,0:T(8,128)S(1)}, u32[]{:S(2)}, u32[]{:S(2)}) collective-permute-start(f32[512,128]{1,0:T(8,128)S(1)} %get-tuple-element.14), channel_id=1, source_target_pairs={{0,4},{4,0},{1,5},{5,1},{2,6},{6,2},{3,7},{7,3},{8,12},{12,8},{9,1... | collective-permute-start | bytes 786440 | tf_op jit(solution)/shard_map/ppermute | solution.py:190

commit v9 on v8

--- a/solution.py
+++ b/solution.py
@@ -108,18 +108,18 @@
         start = pl.multiple_of(table[rows[s], cb] * BLK, BLK)
         return integrals[s * BLK:(s + 1) * BLK, pl.ds(start, BLK)]
 
-    for panels in range(2):
-        result = jnp.zeros((64, 8 * BLK), F32)
+    for panels in range(4):
+        result = jnp.zeros((64, 4 * BLK), F32)
         for s in range(0, 8, 2):
             weights = [
-                jnp.concatenate([block(t, panels * 8 + i) for i in range(8)], axis=1)
+                jnp.concatenate([block(t, panels * 4 + i) for i in range(4)], axis=1)
                 for t in (s, s + 1)
             ]
             result = result + dot(
                 a[:, s * BLK:(s + 2) * BLK], jnp.concatenate(weights, axis=0)
             )
-        for i in range(8):
-            cb = panels * 8 + i
+        for i in range(4):
+            cb = panels * 4 + i
             for h, out in enumerate((own, other)):
                 for r in range(2):
                     at = h * 32 + r * 16
@@ -129,7 +129,8 @@
 
 
 def collect_kernel(spread, recv, out):
-    total = jnp.sum(recv[...], axis=0)
+    parts = [jnp.sum(recv[k * 16:(k + 1) * 16], axis=0) for k in range(4)]
+    total = (parts[0] + parts[1]) + (parts[2] + parts[3])
     places = spread[...]
     for j in range(16):
         line = jnp.where(places[:, j:j + 1] > 0.0, total, 0.0)

time: 39.3 us -> 39.3 us (level)
  no operation moved by 1% of the time
where the time goes in v9:
time: 39.3 us; the launch traced here: 39 us
  blocking collectives  33.4 us (85%)
  Pallas kernels  3.8 us (10%)
  waiting for transfers between devices  1.16 us (3%)
  starting transfers between devices  0.61 us (2%)
    all_to_all x1, blocking collectives, shards(): lax.all_to_all(outgoing.reshape(32, 16, BLK), ('c', 'z', 'x'), split_axis...  17 us
    all_to_all x1, blocking collectives, shards(): lax.all_to_all(chip_sum.reshape(64, 8, BLK), ('y', 'z', 'x'), split_axis=...  16.3 us
    pallas_call x1, Pallas kernels, shards(): pl.pallas_call(route_kernel, out_shape=(jax.ShapeDtypeStruct((512, BLK),...  1.68 us
    pallas_call x1, Pallas kernels, shards(): pl.pallas_call(contract_kernel, out_shape=(jax.ShapeDtypeStruct((512, BLK...  1.4 us
    ppermute x1, waiting for transfers between devices, shards(): chip_sum = own + lax.ppermute(other, 'c', [(0, 1), (1, 0)])  1.16 us
  transfers between devices with their start and end apart: 1, of which 1 were waited for; matrix products, arithmetic and copies ran while one was open for 0% of the time, Pallas kernels for 0%

profile of v9, /device:TPU:1, one launch (start us, length us, event | category | flops | bytes accessed | tf_op | source)
XLA Modules:
  0.0 39.0 jit_solution(3524532456394274154)
XLA Ops:
  0.0 0.0 copy-start
  0.0 1.7 %route.1 = (bf16[512,128]{1,0:T(8,128)(2,1)S(1)}, s32[8,128]{1,0:T(8,128)S(4)}, f32[8,128]{1,0:T(8,128)S(1)}) custom-call(s32[200]{0:T(256)} %occ_h.1, s32[2,64]{1,0:T(2,128)} %bitcast.18, bf16[1024,128]{1,0:T(8,128)(2,1)} %bitcast.15, s32[1,512]{1,0:T(1,128)} %bitcast.16, s32[1,512]{1,0:T(1,128)} %bitcast.17, s32[1,64]{1,0:T(1,128)} %bitcast.19), custom_call_target="tpu_custom_call" | custom-call | flops 42949672960 | bytes 268435456 | tf_op jit(solution)/shard_map/route/pallas_call | solution.py:155
  1.7 17.0 %all_to_all.10 = bf16[32,16,128]{2,1,0:T(8,128)(2,1)S(1)} all-to-all(bf16[32,16,128]{2,1,0:T(8,128)(2,1)S(1)} %bitcast.14), channel_id=1, replica_groups=mesh['z'=4,'x'=4,'c'=2,'y'=4] {'c','z','x'}, dimensions={0} | all-to-all | bytes 262144 | tf_op jit(solution)/shard_map/all_to_all | solution.py:179
  18.7 0.0 copy-done
  18.7 1.4 %contract.1 = (f32[512,128]{1,0:T(8,128)S(1)}, f32[512,128]{1,0:T(8,128)S(1)}) custom-call(s32[8,128]{1,0:T(8,128)S(4)} %get-tuple-element.11.table, bf16[512,128]{1,0:T(8,128)(2,1)S(1)} %bitcast.13, bf16[1024,8192]{1,0:T(8,128)(2,1)S(1)} %copy-done), custom_call_target="tpu_custom_call" | custom-call | tf_op jit(solution)/shard_map/contract/pallas_call | solution.py:182
  20.1 0.6 %collective-permute-start = (f32[512,128]{1,0:T(8,128)S(1)}, f32[512,128]{1,0:T(8,128)S(1)}, u32[]{:S(2)}, u32[]{:S(2)}) collective-permute-start(f32[512,128]{1,0:T(8,128)S(1)} %get-tuple-element.14), channel_id=1, source_target_pairs={{0,4},{4,0},{1,5},{5,1},{2,6},{6,2},{3,7},{7,3},{8,12},{12,8},{9,1... | collective-permute-start | bytes 786440 | tf_op jit(solution)/shard_map/ppermute | solution.py:191
  20.7 1.2 %collective-permute-done = f32[512,128]{1,0:T(8,128)S(1)} collective-permute-done((f32[512,128]{1,0:T(8,128)S(1)}, f32[512,128]{1,0:T(8,128)S(1)}, u32[]{:S(2)}, u32[]{:S(2)}) %collective-permute-start) | collective-permute-done | bytes 262176 | tf_op jit(solution)/shard_map/ppermute | solution.py:191
  21.9 16.3 %all_to_all.11.recv = f32[64,8,128]{2,1,0:T(8,128)S(1)} all-to-all(f32[64,8,128]{2,1,0:T(8,128)S(1)} %add_bitcast_fusion), channel_id=1, replica_groups=mesh['z'=4,'x'=4,'c'=2,'y'=4] {'y','z','x'}, dimensions={0} | all-to-all | bytes 524288 | tf_op jit(solution)/shard_map/all_to_all | solution.py:192
  38.3 0.7 %collect.1 = f32[2,2048]{1,0:T(2,128)} custom-call(f32[8,128]{1,0:T(8,128)S(1)} %get-tuple-element.10.spread, f32[64,8,128]{2,1,0:T(8,128)S(1)} %all_to_all.11.recv), custom_call_target="tpu_custom_call" | custom-call | tf_op jit(solution)/shard_map/collect/pallas_call | solution.py:195
  (1 shorter events, 0.0 us)
Async XLA Ops:
  0.0 18.7 %copy-start = (bf16[1024,8192]{1,0:T(8,128)(2,1)S(1)}, bf16[1024,8192]{1,0:T(8,128)(2,1)}, u32[]{:S(2)}) copy-start(bf16[1024,8192]{1,0:T(8,128)(2,1)} %integrals.1) | copy-start | bytes 50331652
  20.1 1.8 %collective-permute-start = (f32[512,128]{1,0:T(8,128)S(1)}, f32[512,128]{1,0:T(8,128)S(1)}, u32[]{:S(2)}, u32[]{:S(2)}) collective-permute-start(f32[512,128]{1,0:T(8,128)S(1)} %get-tuple-element.14), channel_id=1, source_target_pairs={{0,4},{4,0},{1,5},{5,1},{2,6},{6,2},{3,7},{7,3},{8,12},{12,8},{9,1... | collective-permute-start | bytes 786440 | tf_op jit(solution)/shard_map/ppermute | solution.py:191

commit v10 on v9

--- a/solution.py
+++ b/solution.py
@@ -110,13 +110,13 @@
 
     for panels in range(4):
         result = jnp.zeros((64, 4 * BLK), F32)
-        for s in range(0, 8, 2):
+        for s in range(0, 8, 4):
             weights = [
                 jnp.concatenate([block(t, panels * 4 + i) for i in range(4)], axis=1)
-                for t in (s, s + 1)
+                for t in range(s, s + 4)
             ]
             result = result + dot(
-                a[:, s * BLK:(s + 2) * BLK], jnp.concatenate(weights, axis=0)
+                a[:, s * BLK:(s + 4) * BLK], jnp.concatenate(weights, axis=0)
             )
         for i in range(4):
             cb = panels * 4 + i

time: 39.3 us -> 39.3 us (level)
  no operation moved by 1% of the time
where the time goes in v10:
time: 39.3 us; the launch traced here: 39 us
  blocking collectives  33.4 us (85%)
  Pallas kernels  3.79 us (10%)
  waiting for transfers between devices  1.16 us (3%)
  starting transfers between devices  0.61 us (2%)
    all_to_all x1, blocking collectives, shards(): lax.all_to_all(outgoing.reshape(32, 16, BLK), ('c', 'z', 'x'), split_axis...  17 us
    all_to_all x1, blocking collectives, shards(): lax.all_to_all(chip_sum.reshape(64, 8, BLK), ('y', 'z', 'x'), split_axis=...  16.3 us
    pallas_call x1, Pallas kernels, shards(): pl.pallas_call(route_kernel, out_shape=(jax.ShapeDtypeStruct((512, BLK),...  1.68 us
    pallas_call x1, Pallas kernels, shards(): pl.pallas_call(contract_kernel, out_shape=(jax.ShapeDtypeStruct((512, BLK...  1.39 us
    ppermute x1, waiting for transfers between devices, shards(): chip_sum = own + lax.ppermute(other, 'c', [(0, 1), (1, 0)])  1.16 us
  transfers between devices with their start and end apart: 1, of which 1 were waited for; matrix products, arithmetic and copies ran while one was open for 0% of the time, Pallas kernels for 0%

profile of v10, /device:TPU:1, one launch (start us, length us, event | category | flops | bytes accessed | tf_op | source)
XLA Modules:
  0.0 39.0 jit_solution(15779872489098512408)
XLA Ops:
  0.0 0.0 copy-start
  0.0 1.7 %route.1 = (bf16[512,128]{1,0:T(8,128)(2,1)S(1)}, s32[8,128]{1,0:T(8,128)S(4)}, f32[8,128]{1,0:T(8,128)S(1)}) custom-call(s32[200]{0:T(256)} %occ_h.1, s32[2,64]{1,0:T(2,128)} %bitcast.18, bf16[1024,128]{1,0:T(8,128)(2,1)} %bitcast.15, s32[1,512]{1,0:T(1,128)} %bitcast.16, s32[1,512]{1,0:T(1,128)} %bitcast.17, s32[1,64]{1,0:T(1,128)} %bitcast.19), custom_call_target="tpu_custom_call" | custom-call | flops 42949672960 | bytes 268435456 | tf_op jit(solution)/shard_map/route/pallas_call | solution.py:155
  1.7 17.0 %all_to_all.10 = bf16[32,16,128]{2,1,0:T(8,128)(2,1)S(1)} all-to-all(bf16[32,16,128]{2,1,0:T(8,128)(2,1)S(1)} %bitcast.14), channel_id=1, replica_groups=mesh['z'=4,'x'=4,'c'=2,'y'=4] {'c','z','x'}, dimensions={0} | all-to-all | bytes 262144 | tf_op jit(solution)/shard_map/all_to_all | solution.py:179
  18.7 0.0 copy-done
  18.7 1.4 %contract.1 = (f32[512,128]{1,0:T(8,128)S(1)}, f32[512,128]{1,0:T(8,128)S(1)}) custom-call(s32[8,128]{1,0:T(8,128)S(4)} %get-tuple-element.11.table, bf16[512,128]{1,0:T(8,128)(2,1)S(1)} %bitcast.13, bf16[1024,8192]{1,0:T(8,128)(2,1)S(1)} %copy-done), custom_call_target="tpu_custom_call" | custom-call | tf_op jit(solution)/shard_map/contract/pallas_call | solution.py:182
  20.1 0.6 %collective-permute-start = (f32[512,128]{1,0:T(8,128)S(1)}, f32[512,128]{1,0:T(8,128)S(1)}, u32[]{:S(2)}, u32[]{:S(2)}) collective-permute-start(f32[512,128]{1,0:T(8,128)S(1)} %get-tuple-element.14), channel_id=1, source_target_pairs={{0,4},{4,0},{1,5},{5,1},{2,6},{6,2},{3,7},{7,3},{8,12},{12,8},{9,1... | collective-permute-start | bytes 786440 | tf_op jit(solution)/shard_map/ppermute | solution.py:191
  20.7 1.2 %collective-permute-done = f32[512,128]{1,0:T(8,128)S(1)} collective-permute-done((f32[512,128]{1,0:T(8,128)S(1)}, f32[512,128]{1,0:T(8,128)S(1)}, u32[]{:S(2)}, u32[]{:S(2)}) %collective-permute-start) | collective-permute-done | bytes 262176 | tf_op jit(solution)/shard_map/ppermute | solution.py:191
  21.9 16.3 %all_to_all.11.recv = f32[64,8,128]{2,1,0:T(8,128)S(1)} all-to-all(f32[64,8,128]{2,1,0:T(8,128)S(1)} %add_bitcast_fusion), channel_id=1, replica_groups=mesh['z'=4,'x'=4,'c'=2,'y'=4] {'y','z','x'}, dimensions={0} | all-to-all | bytes 524288 | tf_op jit(solution)/shard_map/all_to_all | solution.py:192
  38.3 0.7 %collect.1 = f32[2,2048]{1,0:T(2,128)} custom-call(f32[8,128]{1,0:T(8,128)S(1)} %get-tuple-element.10.spread, f32[64,8,128]{2,1,0:T(8,128)S(1)} %all_to_all.11.recv), custom_call_target="tpu_custom_call" | custom-call | tf_op jit(solution)/shard_map/collect/pallas_call | solution.py:195
  (1 shorter events, 0.0 us)
Async XLA Ops:
  0.0 18.7 %copy-start = (bf16[1024,8192]{1,0:T(8,128)(2,1)S(1)}, bf16[1024,8192]{1,0:T(8,128)(2,1)}, u32[]{:S(2)}) copy-start(bf16[1024,8192]{1,0:T(8,128)(2,1)} %integrals.1) | copy-start | bytes 50331652
  20.1 1.8 %collective-permute-start = (f32[512,128]{1,0:T(8,128)S(1)}, f32[512,128]{1,0:T(8,128)S(1)}, u32[]{:S(2)}, u32[]{:S(2)}) collective-permute-start(f32[512,128]{1,0:T(8,128)S(1)} %get-tuple-element.14), channel_id=1, source_target_pairs={{0,4},{4,0},{1,5},{5,1},{2,6},{6,2},{3,7},{7,3},{8,12},{12,8},{9,1... | collective-permute-start | bytes 786440 | tf_op jit(solution)/shard_map/ppermute | solution.py:191

commit v11 on v10

--- a/solution.py
+++ b/solution.py
@@ -110,13 +110,13 @@
 
     for panels in range(4):
         result = jnp.zeros((64, 4 * BLK), F32)
-        for s in range(0, 8, 4):
+        for s in range(0, 8, 8):
             weights = [
                 jnp.concatenate([block(t, panels * 4 + i) for i in range(4)], axis=1)
-                for t in range(s, s + 4)
+                for t in range(s, s + 8)
             ]
             result = result + dot(
-                a[:, s * BLK:(s + 4) * BLK], jnp.concatenate(weights, axis=0)
+                a[:, s * BLK:(s + 8) * BLK], jnp.concatenate(weights, axis=0)
             )
         for i in range(4):
             cb = panels * 4 + i

time: 39.3 us -> 39.3 us (level)
  no operation moved by 1% of the time
where the time goes in v11:
time: 39.3 us; the launch traced here: 39 us
  blocking collectives  33.4 us (85%)
  Pallas kernels  3.81 us (10%)
  waiting for transfers between devices  1.16 us (3%)
  starting transfers between devices  0.6 us (2%)
    all_to_all x1, blocking collectives, shards(): lax.all_to_all(outgoing.reshape(32, 16, BLK), ('c', 'z', 'x'), split_axis...  17 us
    all_to_all x1, blocking collectives, shards(): lax.all_to_all(chip_sum.reshape(64, 8, BLK), ('y', 'z', 'x'), split_axis=...  16.3 us
    pallas_call x1, Pallas kernels, shards(): pl.pallas_call(route_kernel, out_shape=(jax.ShapeDtypeStruct((512, BLK),...  1.68 us
    pallas_call x1, Pallas kernels, shards(): pl.pallas_call(contract_kernel, out_shape=(jax.ShapeDtypeStruct((512, BLK...  1.41 us
    ppermute x1, waiting for transfers between devices, shards(): chip_sum = own + lax.ppermute(other, 'c', [(0, 1), (1, 0)])  1.16 us
  transfers between devices with their start and end apart: 1, of which 1 were waited for; matrix products, arithmetic and copies ran while one was open for 0% of the time, Pallas kernels for 0%

profile of v11, /device:TPU:1, one launch (start us, length us, event | category | flops | bytes accessed | tf_op | source)
XLA Modules:
  0.0 39.0 jit_solution(3648137507655984636)
XLA Ops:
  0.0 0.0 copy-start
  0.0 1.7 %route.1 = (bf16[512,128]{1,0:T(8,128)(2,1)S(1)}, s32[8,128]{1,0:T(8,128)S(4)}, f32[8,128]{1,0:T(8,128)S(1)}) custom-call(s32[200]{0:T(256)} %occ_h.1, s32[2,64]{1,0:T(2,128)} %bitcast.18, bf16[1024,128]{1,0:T(8,128)(2,1)} %bitcast.15, s32[1,512]{1,0:T(1,128)} %bitcast.16, s32[1,512]{1,0:T(1,128)} %bitcast.17, s32[1,64]{1,0:T(1,128)} %bitcast.19), custom_call_target="tpu_custom_call" | custom-call | flops 42949672960 | bytes 268435456 | tf_op jit(solution)/shard_map/route/pallas_call | solution.py:155
  1.7 17.0 %all_to_all.10 = bf16[32,16,128]{2,1,0:T(8,128)(2,1)S(1)} all-to-all(bf16[32,16,128]{2,1,0:T(8,128)(2,1)S(1)} %bitcast.14), channel_id=1, replica_groups=mesh['z'=4,'x'=4,'c'=2,'y'=4] {'c','z','x'}, dimensions={0} | all-to-all | bytes 262144 | tf_op jit(solution)/shard_map/all_to_all | solution.py:179
  18.7 0.0 copy-done
  18.7 1.4 %contract.1 = (f32[512,128]{1,0:T(8,128)S(1)}, f32[512,128]{1,0:T(8,128)S(1)}) custom-call(s32[8,128]{1,0:T(8,128)S(4)} %get-tuple-element.11.table, bf16[512,128]{1,0:T(8,128)(2,1)S(1)} %bitcast.13, bf16[1024,8192]{1,0:T(8,128)(2,1)S(1)} %copy-done), custom_call_target="tpu_custom_call" | custom-call | tf_op jit(solution)/shard_map/contract/pallas_call | solution.py:182
  20.1 0.6 %collective-permute-start = (f32[512,128]{1,0:T(8,128)S(1)}, f32[512,128]{1,0:T(8,128)S(1)}, u32[]{:S(2)}, u32[]{:S(2)}) collective-permute-start(f32[512,128]{1,0:T(8,128)S(1)} %get-tuple-element.14), channel_id=1, source_target_pairs={{0,4},{4,0},{1,5},{5,1},{2,6},{6,2},{3,7},{7,3},{8,12},{12,8},{9,1... | collective-permute-start | bytes 786440 | tf_op jit(solution)/shard_map/ppermute | solution.py:191
  20.7 1.2 %collective-permute-done = f32[512,128]{1,0:T(8,128)S(1)} collective-permute-done((f32[512,128]{1,0:T(8,128)S(1)}, f32[512,128]{1,0:T(8,128)S(1)}, u32[]{:S(2)}, u32[]{:S(2)}) %collective-permute-start) | collective-permute-done | bytes 262176 | tf_op jit(solution)/shard_map/ppermute | solution.py:191
  21.9 16.3 %all_to_all.11.recv = f32[64,8,128]{2,1,0:T(8,128)S(1)} all-to-all(f32[64,8,128]{2,1,0:T(8,128)S(1)} %add_bitcast_fusion), channel_id=1, replica_groups=mesh['z'=4,'x'=4,'c'=2,'y'=4] {'y','z','x'}, dimensions={0} | all-to-all | bytes 524288 | tf_op jit(solution)/shard_map/all_to_all | solution.py:192
  38.3 0.7 %collect.1 = f32[2,2048]{1,0:T(2,128)} custom-call(f32[8,128]{1,0:T(8,128)S(1)} %get-tuple-element.10.spread, f32[64,8,128]{2,1,0:T(8,128)S(1)} %all_to_all.11.recv), custom_call_target="tpu_custom_call" | custom-call | tf_op jit(solution)/shard_map/collect/pallas_call | solution.py:195
  (1 shorter events, 0.0 us)
Async XLA Ops:
  0.0 18.7 %copy-start = (bf16[1024,8192]{1,0:T(8,128)(2,1)S(1)}, bf16[1024,8192]{1,0:T(8,128)(2,1)}, u32[]{:S(2)}) copy-start(bf16[1024,8192]{1,0:T(8,128)(2,1)} %integrals.1) | copy-start | bytes 50331652
  20.1 1.8 %collective-permute-start = (f32[512,128]{1,0:T(8,128)S(1)}, f32[512,128]{1,0:T(8,128)S(1)}, u32[]{:S(2)}, u32[]{:S(2)}) collective-permute-start(f32[512,128]{1,0:T(8,128)S(1)} %get-tuple-element.14), channel_id=1, source_target_pairs={{0,4},{4,0},{1,5},{5,1},{2,6},{6,2},{3,7},{7,3},{8,12},{12,8},{9,1... | collective-permute-start | bytes 786440 | tf_op jit(solution)/shard_map/ppermute | solution.py:191
